TPU v7x, 512 devices: a whole 4x8x8 slice. The times are simulated.
512 devices in a mesh: dp: 64 (over x, z, core), tp: 8 (over y).
Axes of the slice: x: 4, y: 8, z: 8, core: 2. Of those that a mesh axis runs over, the one named last changes fastest.
Arguments:
- normed_layer_input: bfloat16 [18432, 7168], P('dp', 'tp'), may hold values from -6 to 6
- queries: bfloat16 [16384, 7168], P('dp', 'tp'), may hold values from -100 to 100
- saved_key_rows: bfloat16 [18432, 1024], P('dp', 'tp'), may hold values from -4.5 to 4.5
- saved_value_rows: bfloat16 [18432, 1024], P('dp', 'tp'), may hold values from -6 to 6
- attention_output_gradient: bfloat16 [16384, 7168], P('dp', 'tp'), may hold values from -6 to 6
- finisher_token_mask: int32 [16384], P('dp'), may hold values 0 or 1
- response_length: int32 [64], P('dp'), may hold values from 128 to 256
- value_weight_matrix: bfloat16 [1024, 7168], P('tp'), may hold values from -0.0625 to 0.0625
- adapter_down_factor: bfloat16 [7168, 64], P('tp'), may hold values from -0.0625 to 0.0625
- adapter_up_factor: bfloat16 [64, 1024], P(None, 'tp'), may hold values from -0.75 to 0.75
Outputs:
- layer_input_gradient: bfloat16 [18432, 7168], P('dp', 'tp')
- query_grad: bfloat16 [16384, 7168], P('dp', 'tp')
- key_grad: bfloat16 [18432, 1024], P('dp', 'tp')
- down_factor_gradient: float32 [7168, 64], P('tp')
- up_factor_gradient: float32 [64, 1024], P(None, 'tp')
All inputs are finite; a program needn't handle non-finite values. No bound on the sum of `finisher_token_mask` on one device may be relied on, other than what follows from the above.
Results may differ from a plain program's by a relative error of at most 0.02.
Values may be sent and summed in bfloat16 or wider, within the bound.
A program may use at most 64 MiB of HBM per device.

v0:
```python
import math

import jax
import jax.numpy as jnp
from jax import lax
from jax.sharding import PartitionSpec as P

QH = 56
KVH = 8
HD = 128


adapter_scale = 2.0


def attend_back(queries, saved_key_rows, saved_value_rows, attention_output_gradient, keep, length):
    replies = queries.shape[0]
    context = saved_key_rows.shape[0]
    prompt = context - replies
    local_heads = saved_key_rows.shape[1] // HD
    group_size = QH // KVH
    factor = 1.0 / math.sqrt(HD)
    q_heads = queries.reshape(replies, local_heads, group_size, HD)
    k_heads = saved_key_rows.reshape(context, local_heads, HD)
    v_heads = saved_value_rows.reshape(context, local_heads, HD)
    grad_rows = (attention_output_gradient * keep[:, None]).reshape(
        replies, local_heads, group_size, HD
    )
    row_ids = jnp.arange(replies, dtype=jnp.int32)[:, None]
    col_ids = jnp.arange(context, dtype=jnp.int32)[None, :]
    visible = (col_ids <= prompt + row_ids) & ((col_ids < prompt) | (col_ids - prompt < length))
    scores = (
        jnp.einsum("rxgd,cxd->xgrc", q_heads, k_heads, preferred_element_type=jnp.float32) * factor
    )
    scores = jnp.where(visible[None, None], scores, -1e30)
    top = jnp.max(scores, axis=-1, keepdims=True)
    expo = jnp.exp(scores - top)
    probs = expo / jnp.sum(expo, axis=-1, keepdims=True)
    probs_low = probs.astype(jnp.bfloat16)
    dprobs = jnp.einsum("rxgd,cxd->xgrc", grad_rows, v_heads, preferred_element_type=jnp.float32)
    dscores = probs * (dprobs - jnp.sum(probs * dprobs, axis=-1, keepdims=True)) * factor
    dscores_low = dscores.astype(jnp.bfloat16)
    query_grad = jnp.einsum(
        "xgrc,cxd->rxgd", dscores_low, k_heads, preferred_element_type=jnp.float32
    )
    key_grad = jnp.einsum(
        "xgrc,rxgd->cxd", dscores_low, q_heads, preferred_element_type=jnp.float32
    )
    value_rows_gradient = jnp.einsum(
        "xgrc,rxgd->cxd", probs_low, grad_rows, preferred_element_type=jnp.float32
    )
    return (
        query_grad.reshape(replies, -1).astype(jnp.bfloat16),
        key_grad.reshape(context, -1).astype(jnp.bfloat16),
        value_rows_gradient.reshape(context, -1).astype(jnp.bfloat16),
    )


def per_device(
    normed_layer_input,
    queries,
    saved_key_rows,
    saved_value_rows,
    attention_output_gradient,
    finisher_token_mask,
    response_length,
    value_weight_matrix,
    adapter_down_factor,
    adapter_up_factor,
):
    replies = queries.shape[0]
    length = response_length[0]
    row_ids = jnp.arange(replies, dtype=jnp.int32)
    keep = jnp.where(row_ids < length, finisher_token_mask, 0).astype(jnp.bfloat16)
    down_partial_gradient = jnp.dot(
        normed_layer_input, adapter_down_factor, preferred_element_type=jnp.float32
    )
    down_sum = lax.psum(down_partial_gradient.astype(jnp.bfloat16), "tp")
    query_grad, key_grad, value_rows_gradient = attend_back(
        queries, saved_key_rows, saved_value_rows, attention_output_gradient, keep, length
    )
    up_part = lax.dot_general(
        value_rows_gradient,
        adapter_up_factor,
        (((1,), (1,)), ((), ())),
        preferred_element_type=jnp.float32,
    )
    up_sum = lax.psum(up_part.astype(jnp.bfloat16), "tp")
    partial_term = jnp.dot(
        value_rows_gradient, value_weight_matrix, preferred_element_type=jnp.float32
    )
    frozen_value_output = lax.psum_scatter(
        partial_term.astype(jnp.bfloat16), "tp", scatter_dimension=1, tiled=True
    ).astype(jnp.float32)
    adapter_contribution = lax.dot_general(
        up_sum, adapter_down_factor, (((1,), (1,)), ((), ())), preferred_element_type=jnp.float32
    )
    layer_input_gradient = (frozen_value_output + adapter_scale * adapter_contribution).astype(
        jnp.bfloat16
    )
    down_shard_gradient = adapter_scale * lax.dot_general(
        normed_layer_input, up_sum, (((0,), (0,)), ((), ())), preferred_element_type=jnp.float32
    )
    up_shard_gradient = adapter_scale * lax.dot_general(
        down_sum, value_rows_gradient, (((0,), (0,)), ((), ())), preferred_element_type=jnp.float32
    )
    down_factor_gradient, up_factor_gradient = lax.psum(
        (down_shard_gradient, up_shard_gradient), "dp"
    )
    return (layer_input_gradient, query_grad, key_grad, down_factor_gradient, up_factor_gradient)


def solution(mesh):
    in_specs = (
        P("dp", "tp"),
        P("dp", "tp"),
        P("dp", "tp"),
        P("dp", "tp"),
        P("dp", "tp"),
        P("dp"),
        P("dp"),
        P("tp", None),
        P("tp", None),
        P(None, "tp"),
    )
    out_specs = (P("dp", "tp"), P("dp", "tp"), P("dp", "tp"), P("tp", None), P(None, "tp"))
    return jax.shard_map(
        per_device, mesh=mesh, in_specs=in_specs, out_specs=out_specs, check_vma=False
    )
```

profile of v0, /device:TPU:1, one launch (start us, length us, event | category | flops | bytes accessed | tf_op | source)
XLA Modules:
  0.0 531.8 jit_solution(3073473745786576381)
XLA Ops:
  7.2 0.0 copy-start
  7.2 0.0 all-reduce.6.cloned.1.call-start
  7.2 1.3 copy.28
  9.3 1.2 copy.27
  10.5 0.1 fusion.15
  10.6 0.0 copy-start.8
  10.6 1.3 fusion.23
  12.0 0.0 copy-start.1
  12.0 0.3 fusion.5
  12.3 0.0 copy-done.8
  12.3 0.0 copy-start.7
  12.3 0.0 copy-start.3
  12.3 0.0 copy-start.4
  12.4 0.5 fusion.11
  12.8 0.4 copy-done.1
  13.3 0.0 copy-done.7
  13.3 0.8 convolution_convert_fusion.3
  14.0 0.0 copy-done.3
  14.1 0.0 copy-done.4
  14.1 0.9 convolution_convert_fusion.2
  15.0 0.0 all-reduce.6.cloned.1.call-update
  15.0 0.0 reduce-scatter.4.cloned.1.call-start
  15.1 0.0 copy-done
  15.1 3.2 convolution_convert_fusion
  18.3 7.3 %copy.38 = bf16[288,7168]{0,1:T(8,128)(2,1)} copy(bf16[288,7168]{1,0:T(8,128)(2,1)} %convolution_convert_fusion) | data formatting | bytes 8257536
  25.6 0.0 copy-start.9
  25.6 0.0 reduce-scatter.4.cloned.1.call-update
  25.7 0.0 all-reduce.4.cloned.1.call-start
  25.7 0.8 copy-done.9
  26.5 0.0 copy-start.2
  26.5 2.3 fusion
  28.8 0.0 copy-done.2
  28.8 0.0 copy-start.5
  28.8 0.6 fusion.12
  29.4 0.3 copy-done.5
  29.7 1.2 convolution_convert_fusion.1
  30.9 2.0 copy.33
  32.9 1.1 fusion.10
  34.0 58.9 %all-reduce.6.cloned.1.call-done = (bf16[288,64]{0,1:T(8,128)(2,1)}, bf16[288,64]{0,1:T(8,128)(2,1)}) async-done(((bf16[288,64]{0,1:T(8,128)(2,1)}, bf16[288,64]{0,1:T(8,128)(2,1)}), (bf16[288,64]{0,1:T(8,128)(2,1)}, bf16[288,64]{0,1:T(8,128)(2,1)})) %all-reduce.6.cloned.1.call-update) | async-done | bytes 73744 | tf_op jit(solution)/shard_map/psum | solution.py:88
  92.9 0.0 copy-start.6
  92.9 0.9 convolution_multiply_fusion.2
  93.8 247.2 %psum.31 = f32[64,128]{1,0:T(8,128)} all-reduce(f32[64,128]{1,0:T(8,128)S(1)} %convolution_multiply_fusion.2), channel_id=1, replica_groups=mesh['dp'=64,'tp'=8] {'dp'}, use_global_device_ids=true, to_apply=%region_7.8 | all-reduce | flops 8192 | bytes 65536 | tf_op jit(solution)/shard_map/psum | solution.py:107
  341.0 2.0 fusion.8
  343.0 0.0 all-reduce.4.cloned.1.call-update
  343.1 0.0 reduce-scatter.4.cloned.1.call-done
  343.1 1.4 copy.39
  344.5 0.0 copy-done.6
  344.5 1.1 fusion.7
  345.6 178.0 %all-reduce.4.cloned.1.call-done = f32[896,64]{0,1:T(8,128)} async-done(((f32[896,64]{0,1:T(8,128)}), f32[896,64]{0,1:T(8,128)}) %all-reduce.4.cloned.1.call-update) | async-done | bytes 229392 | tf_op jit(solution)/shard_map/psum | solution.py:107
  523.6 1.6 copy.44
  (4 shorter events, 0.1 us)
Async XLA Ops:
  7.2 7.9 %copy-start = (bf16[128,7168]{1,0:T(8,128)(2,1)S(1)}, bf16[128,7168]{1,0:T(8,128)(2,1)}, u32[]{:S(2)}) copy-start(bf16[128,7168]{1,0:T(8,128)(2,1)} %param.17) | copy-start | bytes 5505028
  7.2 85.7 %all-reduce.6.cloned.1.call-start = ((), (), s32[]{:S(2)}) async-start(), calls=%async_computation.3 | async-start | bytes 196608 | tf_op jit(solution)/shard_map/psum | solution.py:88
  10.6 1.7 copy-start.8
  12.0 1.3 copy-start.1
  12.3 0.9 copy-start.7
  12.3 1.7 copy-start.3
  12.3 1.7 copy-start.4
  15.0 328.1 %reduce-scatter.4.cloned.1.call-start = ((), (), s32[]{:S(2)}) async-start(), calls=%async_computation.2 | async-start | bytes 6193152
  25.6 0.9 copy-start.9
  25.7 498.0 %all-reduce.4.cloned.1.call-start = ((), (), s32[]{:S(2)}) async-start(), calls=%async_computation.1 | async-start | bytes 458752 | tf_op jit(solution)/shard_map/psum | solution.py:107
  26.5 2.3 copy-start.2
  28.8 0.9 copy-start.5
  92.9 251.6 %copy-start.6 = (bf16[288,64]{0,1:T(8,128)(2,1)S(1)}, bf16[288,64]{0,1:T(8,128)(2,1)}, u32[]{:S(2)}) copy-start(bf16[288,64]{0,1:T(8,128)(2,1)} %get-tuple-element.20) | copy-start | bytes 110596
Sparse Core Ops, SparseCore 0:
  15.1 77.7 all-reduce.5
  96.0 73.3 reduce-scatter.3
  343.2 180.4 all-reduce.3
where the time goes:
time: 532 us
  blocking collectives  247 us (46%)
  waiting for transfers between devices  237 us (45%)
  local copies, waits for them, and re-layouts  16.5 us (3%)
  matrix products  15.3 us (3%)
  between operations  14.6 us (3%)
    psum x1, blocking collectives, per_device(): lax.psum((down_shard_gradient, up_shard_gradient), 'dp')  247 us
    psum x1, waiting for transfers between devices, per_device(): lax.psum((down_shard_gradient, up_shard_gradient), 'dp')  178 us
    psum x1, waiting for transfers between devices, per_device(): up_sum = lax.psum(up_part.astype(jnp.bfloat16), 'tp')  58.9 us
    unnamed x26, local copies, waits for them, and re-layouts  16.5 us
  transfers between devices with their start and end apart: 3, of which 2 were waited for; matrix products, arithmetic and copies ran while one was open for 4% of the time, Pallas kernels for 0%

commit v1 on v0

v1 whole, which is shorter than its diff:
```python
import math

import jax
import jax.numpy as jnp
from jax import lax
from jax.experimental import pallas as pl
from jax.experimental.pallas import tpu as pltpu
from jax.sharding import PartitionSpec as P

MESH = pl.DeviceIdType.MESH
BF16 = jnp.bfloat16
F32 = jnp.float32

QH = 56
KVH = 8
HD = 128
HEADS = QH // KVH
RESP = 256
CTX = 288
PROMPT = CTX - RESP
RANK = 64
FEATS = 896
FACTOR = 1.0 / math.sqrt(HD)
LOG2E = math.log2(math.e)
adapter_scale = 2.0

NX, NZ, NC, NY = 4, 8, 2, 8
ROWS = 16

RB = 128
SEEN = (PROMPT + RB, CTX)

NT = (((1,), (1,)), ((), ()))


def dot(a, b):
    return jnp.dot(a, b, preferred_element_type=F32)


def dot_nt(a, b):
    return lax.dot_general(a, b, NT, preferred_element_type=F32)


def rows_of_heads(ref, b):
    return jnp.concatenate(
        [ref[b * RB : (b + 1) * RB, h * HD : (h + 1) * HD] for h in range(HEADS)], axis=0
    )


def kernel(
    x_hbm, q_hbm, k_hbm, v_hbm, g_hbm, mask_ref, length_ref, w_hbm, at_hbm, b_hbm,
    lig_ref, qg_ref, kg_ref, dfg_ref, ufg_ref,
    x_ref, q_ref, k_ref, v_ref, g_ref, at_ref,
    wfull, bfull, vgfull,
    p0, p1, pb0, pb1,
    dpart, dpieces, dfull,
    rs_src, rs_dst, bc_buf, ag_buf,
    load_sem, w1_send, w1_recv, wz_send, wz_recv, wx_send, wx_recv, wc_send, wc_recv,
    b_send, b_recv, d1_send, d1_recv, d2_send, d2_recv, vg_send, vg_recv,
    rs_send, rs_recv, bc_send, bc_recv, ag_send, ag_recv,
):
    dp = lax.axis_index("dp")
    y = lax.axis_index("tp")
    x = dp // (NZ * NC)
    z = (dp // NC) % NZ
    c = dp % NC

    def at(px, pz, pc, py):
        return {"dp": (px * NZ + pz) * NC + pc, "tp": py}

    y_to = [(y + k) % NY for k in range(1, NY)]
    y_from = [(y + NY - k) % NY for k in range(1, NY)]
    z_to = [(z + k) % NZ for k in range(1, NZ)]
    z_from = [(z + NZ - k) % NZ for k in range(1, NZ)]
    x_to = [(x + k) % NX for k in range(1, NX)]
    x_from = [(x + NX - k) % NX for k in range(1, NX)]
    xc_steps = [(i, j) for i in range(NX) for j in range(NC) if i or j]
    xc_to = [((x + i) % NX, (c + j) % NC) for i, j in xc_steps]
    xc_from = [((x + NX - i) % NX, (c + NC - j) % NC) for i, j in xc_steps]
    y_dev = [at(x, z, c, j) for j in y_to]
    z_dev = [at(x, j, c, y) for j in z_to]
    x_dev = [at(j, z, c, y) for j in x_to]
    xc_dev = [at(i, z, j, y) for i, j in xc_to]
    sibling = at(x, z, 1 - c, y)

    def remote(src, dst, send, recv, device):
        return pltpu.make_async_remote_copy(
            src_ref=src, dst_ref=dst, send_sem=send, recv_sem=recv, device_id=device, device_id_type=MESH
        )

    pending = []

    def fan_out(src, dst, send, recv, devices):
        for k, device in enumerate(devices):
            copy = remote(src(k), dst, send.at[k], recv.at[k], device)
            copy.start()
            pending.append(copy)

    def landed(dst, send, recv, devices):
        for k, device in enumerate(devices):
            remote(dst(k), dst(k), send.at[k], recv.at[k], device).wait_recv()

    barrier = pltpu.get_barrier_semaphore()
    everyone = y_dev + z_dev + xc_dev
    for device in everyone:
        pl.semaphore_signal(barrier, inc=1, device_id=device, device_id_type=MESH)

    w_y = 4 * c + x
    w_rows = pl.ds(pl.multiple_of(z * ROWS, ROWS), ROWS)

    def w_cols(j):
        return pl.ds(pl.multiple_of(j * FEATS, 128), FEATS)

    loads = [
        pltpu.make_async_copy(src, dst, load_sem.at[i])
        for i, (src, dst) in enumerate(
            [
                (x_hbm, x_ref),
                (at_hbm, at_ref),
                (k_hbm, k_ref),
                (q_hbm, q_ref),
                (g_hbm, g_ref),
                (v_hbm, v_ref),
                (b_hbm, bfull.at[y]),
            ]
        )
    ]
    for load in loads:
        load.start()
    load_x, load_a, load_k, load_q, load_g, load_v, load_b = loads
    w_own = pltpu.make_async_copy(w_hbm.at[w_rows, w_cols(y)], wfull.at[w_y, z], load_sem.at[7])

    @pl.when(y == w_y)
    def _():
        w_own.start()

    load_x.wait()
    load_a.wait()
    dpart[...] = dot_nt(at_ref[...], x_ref[...]).reshape(dpart.shape)
    load_b.wait()

    pl.semaphore_wait(barrier, len(everyone))

    @pl.when(y == w_y)
    def _():
        for k in range(NY - 1):
            remote(
                w_hbm.at[w_rows, w_cols(y_to[k])], wfull.at[w_y, z], w1_send.at[k], w1_recv, y_dev[k]
            ).start()

    fan_out(lambda k: dpart.at[y_to[k]], dpieces.at[y], d1_send, d1_recv, y_dev)
    fan_out(lambda k: bfull.at[y], bfull.at[y], b_send, b_recv, y_dev)

    load_k.wait()
    load_q.wait()
    limit = PROMPT - 1 + length_ref[0]
    probs = (p0, p1)
    probs_low = (pb0, pb1)

    def weigh(b, h):
        seen = SEEN[b]
        q = q_ref[b * RB : (b + 1) * RB, h * HD : (h + 1) * HD]
        scores = dot_nt(k_ref[:seen, :], q) * (FACTOR * LOG2E)
        col = lax.broadcasted_iota(jnp.int32, (seen, RB), 0)
        row = lax.broadcasted_iota(jnp.int32, (1, RB), 1) + b * RB
        last = jnp.minimum(row + PROMPT, limit)
        scores = jnp.where(col <= last, scores, -1e30)
        top = jnp.max(scores, axis=0, keepdims=True)
        expo = jnp.exp2(scores - top)
        keep = jnp.where(row + PROMPT <= limit, mask_ref[:, b * RB : (b + 1) * RB], 0).astype(F32)
        p = expo * (keep / jnp.sum(expo, axis=0, keepdims=True))
        probs[b][:, h * HD : (h + 1) * HD] = p
        probs_low[b][:, h * HD : (h + 1) * HD] = p.astype(BF16)

    for h in range(HEADS):
        for b in range(2):
            weigh(b, h)
        if h == 1:
            @pl.when(y == w_y)
            def _():
                w_own.wait()

            @pl.when(y != w_y)
            def _():
                remote(wfull.at[w_y, z], wfull.at[w_y, z], w1_send.at[0], w1_recv, y_dev[0]).wait_recv()

            fan_out(lambda k: wfull.at[w_y, z], wfull.at[w_y, z], wz_send, wz_recv, z_dev)
        if h == 3:
            landed(lambda k: dpieces.at[y_from[k]], d1_send, d1_recv, y_dev)
            total = dpart[y]
            for k in range(NY - 1):
                total = total + dpieces[y_from[k]]
            dfull[y] = total
            fan_out(lambda k: dfull.at[y], dfull.at[y], d2_send, d2_recv, y_dev)
        if h == 5:
            landed(lambda k: wfull.at[w_y, z_from[k]], wz_send, wz_recv, z_dev)
            fan_out(lambda k: wfull.at[w_y], wfull.at[w_y], wx_send, wx_recv, x_dev)

    load_g.wait()
    early = dot(pb0[...], rows_of_heads(g_ref, 0))
    late = dot(pb1[...], rows_of_heads(g_ref, 1))
    vgfull[y, : SEEN[0], :] = (early + late[: SEEN[0]]).astype(BF16)
    vgfull[y, SEEN[0] :, :] = late[SEEN[0] :].astype(BF16)
    fan_out(lambda k: vgfull.at[y], vgfull.at[y], vg_send, vg_recv, y_dev)

    load_v.wait()
    for h in range(HEADS):
        for b in range(2):
            seen = SEEN[b]
            lanes = slice(h * HD, (h + 1) * HD)
            p = probs[b][:, lanes]
            t = p * dot_nt(v_ref[:seen, :], g_ref[b * RB : (b + 1) * RB, lanes])
            probs_low[b][:, lanes] = ((t - p * jnp.sum(t, axis=0, keepdims=True)) * FACTOR).astype(BF16)

    early = dot(pb0[...], rows_of_heads(q_ref, 0))
    late = dot(pb1[...], rows_of_heads(q_ref, 1))
    kg_ref[: SEEN[0], :] = (early + late[: SEEN[0]]).astype(BF16)
    kg_ref[SEEN[0] :, :] = late[SEEN[0] :].astype(BF16)
    keys_t = k_ref[...].astype(F32).T.astype(BF16)
    for b in range(2):
        qg_t = dot(keys_t[:, : SEEN[b]], probs_low[b][...])
        for h in range(HEADS):
            lanes = slice(h * HD, (h + 1) * HD)
            qg_ref[b * RB : (b + 1) * RB, lanes] = qg_t[:, lanes].T.astype(BF16)

    landed(lambda k: dfull.at[y_from[k]], d2_send, d2_recv, y_dev)
    rs_src[NZ - 1] = dot(dfull[...].reshape(RANK, CTX).astype(BF16), vgfull[y]).astype(BF16)

    landed(lambda k: wfull.at[4 * c + x_from[k]], wx_send, wx_recv, x_dev)
    half = pl.ds(4 * c, 4)
    other = pl.ds(4 * (1 - c), 4)
    to_sibling = remote(wfull.at[half], wfull.at[half], wc_send.at[0], wc_recv.at[0], sibling)
    to_sibling.start()

    landed(lambda k: bfull.at[y_from[k]], b_send, b_recv, y_dev)
    landed(lambda k: vgfull.at[y_from[k]], vg_send, vg_recv, y_dev)
    values = jnp.concatenate([vgfull[j] for j in range(NY)], axis=1)
    ups = jnp.concatenate([bfull[j] for j in range(NY)], axis=1)
    up_t = dot_nt(ups, values).astype(BF16)
    dfg_t = dot(up_t, x_ref[...])
    for j in range(NZ - 1):
        rs_src[j] = dfg_t[:, j * 128 : (j + 1) * 128].astype(BF16)

    fan_out(lambda k: rs_src.at[z_to[k]], rs_dst.at[z], rs_send, rs_recv, z_dev)

    up = dot_nt(values, ups).astype(BF16)
    remote(wfull.at[other], wfull.at[other], wc_send.at[0], wc_recv.at[0], sibling).wait_recv()

    def input_gradient(low, high):
        w = wfull[:, :, :, low:high].reshape(NY * HD, high - low)
        frozen = dot(values, w)
        adapter = dot(up, at_ref[:, low:high])
        lig_ref[:, low:high] = (frozen + adapter_scale * adapter).astype(BF16)

    input_gradient(0, 256)

    landed(lambda k: rs_dst.at[z_from[k]], rs_send, rs_recv, z_dev)
    total = rs_src[z].astype(F32)
    for k in range(NZ - 1):
        total = total + rs_dst[z_from[k]].astype(F32)
    bc_buf[x * NC + c] = total.astype(BF16)
    fan_out(lambda k: bc_buf.at[x * NC + c], bc_buf.at[x * NC + c], bc_send, bc_recv, xc_dev)

    input_gradient(256, 512)

    landed(lambda k: bc_buf.at[xc_from[k][0] * NC + xc_from[k][1]], bc_send, bc_recv, xc_dev)
    total = bc_buf[0].astype(F32)
    for j in range(1, NX * NC):
        total = total + bc_buf[j].astype(F32)
    ag_buf[z] = total.astype(BF16)
    fan_out(lambda k: ag_buf.at[z], ag_buf.at[z], ag_send, ag_recv, z_dev)

    input_gradient(512, 896)

    landed(lambda k: ag_buf.at[z_from[k]], ag_send, ag_recv, z_dev)
    for j in range(NZ - 1):
        dfg_ref[:, j * 128 : (j + 1) * 128] = adapter_scale * ag_buf[j].astype(F32)
    ufg_ref[...] = adapter_scale * ag_buf[NZ - 1].astype(F32)

    for copy in pending:
        copy.wait_send()
    to_sibling.wait_send()

    @pl.when(y == w_y)
    def _():
        for k in range(NY - 1):
            remote(
                w_hbm.at[w_rows, w_cols(y_to[k])], wfull.at[w_y, z], w1_send.at[k], w1_recv, y_dev[k]
            ).wait_send()


def per_device(
    normed_layer_input,
    queries,
    saved_key_rows,
    saved_value_rows,
    attention_output_gradient,
    finisher_token_mask,
    response_length,
    value_weight_matrix,
    adapter_down_factor,
    adapter_up_factor,
):
    hbm = pl.BlockSpec(memory_space=pl.ANY)
    vmem = pl.BlockSpec(memory_space=pltpu.VMEM)
    smem = pl.BlockSpec(memory_space=pltpu.SMEM)
    dma = pltpu.SemaphoreType.DMA
    lig, qg, kg, dfg_t, ufg = pl.pallas_call(
        kernel,
        out_shape=(
            jax.ShapeDtypeStruct((CTX, FEATS), BF16),
            jax.ShapeDtypeStruct((RESP, FEATS), BF16),
            jax.ShapeDtypeStruct((CTX, HD), BF16),
            jax.ShapeDtypeStruct((RANK, FEATS), F32),
            jax.ShapeDtypeStruct((RANK, HD), F32),
        ),
        in_specs=[hbm, hbm, hbm, hbm, hbm, vmem, smem, hbm, hbm, hbm],
        out_specs=(vmem,) * 5,
        scratch_shapes=[
            pltpu.VMEM((CTX, FEATS), BF16),
            pltpu.VMEM((RESP, FEATS), BF16),
            pltpu.VMEM((CTX, HD), BF16),
            pltpu.VMEM((CTX, HD), BF16),
            pltpu.VMEM((RESP, FEATS), BF16),
            pltpu.VMEM((RANK, FEATS), BF16),
            pltpu.VMEM((NY, NZ, ROWS, FEATS), BF16),
            pltpu.VMEM((NY, RANK, HD), BF16),
            pltpu.VMEM((NY, CTX, HD), BF16),
            pltpu.VMEM((SEEN[0], FEATS), F32),
            pltpu.VMEM((SEEN[1], FEATS), F32),
            pltpu.VMEM((SEEN[0], FEATS), BF16),
            pltpu.VMEM((SEEN[1], FEATS), BF16),
            pltpu.VMEM((NY, RANK // NY, CTX), F32),
            pltpu.VMEM((NY, RANK // NY, CTX), F32),
            pltpu.VMEM((NY, RANK // NY, CTX), F32),
            pltpu.VMEM((NZ, RANK, HD), BF16),
            pltpu.VMEM((NZ, RANK, HD), BF16),
            pltpu.VMEM((NX * NC, RANK, HD), BF16),
            pltpu.VMEM((NZ, RANK, HD), BF16),
            dma((8,)),
            dma((NY - 1,)),
            dma,
            dma((NZ - 1,)),
            dma((NZ - 1,)),
            dma((NX - 1,)),
            dma((NX - 1,)),
            dma((1,)),
            dma((1,)),
            dma((NY - 1,)),
            dma((NY - 1,)),
            dma((NY - 1,)),
            dma((NY - 1,)),
            dma((NY - 1,)),
            dma((NY - 1,)),
            dma((NY - 1,)),
            dma((NY - 1,)),
            dma((NZ - 1,)),
            dma((NZ - 1,)),
            dma((NX * NC - 1,)),
            dma((NX * NC - 1,)),
            dma((NZ - 1,)),
            dma((NZ - 1,)),
        ],
        compiler_params=pltpu.CompilerParams(
            collective_id=0, has_side_effects=True, vmem_limit_bytes=40 * 1024 * 1024
        ),
    )(
        normed_layer_input,
        queries,
        saved_key_rows,
        saved_value_rows,
        attention_output_gradient,
        finisher_token_mask.reshape(1, RESP),
        response_length,
        value_weight_matrix,
        adapter_down_factor.T,
        adapter_up_factor,
    )
    return (lig, qg, kg, dfg_t.T, ufg)


def solution(mesh):
    in_specs = (
        P("dp", "tp"),
        P("dp", "tp"),
        P("dp", "tp"),
        P("dp", "tp"),
        P("dp", "tp"),
        P("dp"),
        P("dp"),
        P("tp", None),
        P("tp", None),
        P(None, "tp"),
    )
    out_specs = (P("dp", "tp"), P("dp", "tp"), P("dp", "tp"), P("tp", None), P(None, "tp"))
    return jax.shard_map(
        per_device, mesh=mesh, in_specs=in_specs, out_specs=out_specs, check_vma=False
    )
```

time: 532 us -> 76.4 us (0.14)
  blocking collectives: 247 us -> 0 us
  waiting for transfers between devices: 237 us -> 0 us
  Pallas kernels: 0 us -> 62.5 us
  matrix products: 15.3 us -> 0 us
  between operations: 14.6 us -> 1.31 us
    psum x1 -> x0, blocking collectives: 247 us -> none  [per_device(): lax.psum((down_shard_gradient, up_shard_gradient), 'dp')]
    psum x2 -> x0, waiting for transfers between devices: 237 us -> none  [the longest x1 178 us: per_device(): lax.psum((down_shard_gradient, up_shard_gradient), 'dp')]
    pallas_call x0 -> x1, Pallas kernels: none -> 62.5 us  [per_device(): pl.pallas_call(kernel, out_shape=(jax.ShapeDtypeStruct((CTX, FEATS), BF16...]
    dot_general x11 -> x0, matrix products: 15.3 us -> none  [the longest x1 3.24 us: per_device(): jnp.dot(value_rows_gradient, value_weight_matrix, preferred_element_type=...]
    unnamed x26 -> x23, local copies, waits for them, and re-layouts: 16.5 us -> 12.1 us
  transfers between devices with their start and end apart: 3 -> 0, of which waited for: 2 -> 0; matrix products, arithmetic and copies ran while one was open for 4% -> 0% of each run, Pallas kernels for 0% -> 0%
where the time goes in v1:
time: 76.4 us; the launch traced here: 75.9 us
  Pallas kernels  62.5 us (82%)
  local copies, waits for them, and re-layouts  12.1 us (16%)
  between operations  1.31 us (2%)
    pallas_call x1, Pallas kernels, per_device(): pl.pallas_call(kernel, out_shape=(jax.ShapeDtypeStruct((CTX, FEATS), BF16...  62.5 us
    unnamed x23, local copies, waits for them, and re-layouts  12.1 us

profile of v1, /device:TPU:1, one launch (start us, length us, event | category | flops | bytes accessed | tf_op | source)
XLA Modules:
  0.0 75.9 jit_solution(8589854513057991985)
XLA Ops:
  1.3 0.0 copy-start
  1.3 1.5 %copy-done = bf16[128,7168]{1,0:T(8,128)(2,1)S(1)} copy-done((bf16[128,7168]{1,0:T(8,128)(2,1)S(1)}, bf16[128,7168]{1,0:T(8,128)(2,1)}, u32[]{:S(2)}) %copy-start) | copy-done | bytes 1835032
  2.8 0.0 copy-start.1
  2.8 1.0 %copy-done.1 = bf16[288,896]{1,0:T(8,128)(2,1)S(1)} copy-done((bf16[288,896]{1,0:T(8,128)(2,1)S(1)}, bf16[288,896]{1,0:T(8,128)(2,1)}, u32[]{:S(2)}) %copy-start.1) | copy-done | bytes 516120
  3.8 0.0 copy-start.2
  3.8 1.0 %copy-done.2 = bf16[256,896]{1,0:T(8,128)(2,1)S(1)} copy-done((bf16[256,896]{1,0:T(8,128)(2,1)S(1)}, bf16[256,896]{1,0:T(8,128)(2,1)}, u32[]{:S(2)}) %copy-start.2) | copy-done | bytes 458776
  4.8 0.0 copy-start.3
  4.8 1.0 %copy-done.3 = bf16[256,896]{1,0:T(8,128)(2,1)S(1)} copy-done((bf16[256,896]{1,0:T(8,128)(2,1)S(1)}, bf16[256,896]{1,0:T(8,128)(2,1)}, u32[]{:S(2)}) %copy-start.3) | copy-done | bytes 458776
  5.9 0.0 copy-start.4
  5.9 0.9 %copy-done.4 = bf16[896,64]{0,1:T(8,128)(2,1)S(1)} copy-done((bf16[896,64]{0,1:T(8,128)(2,1)S(1)}, bf16[896,64]{0,1:T(8,128)(2,1)}, u32[]{:S(2)}) %copy-start.4) | copy-done | bytes 114712
  6.8 0.0 copy-start.5
  6.8 0.9 %copy-done.5 = bf16[288,128]{1,0:T(8,128)(2,1)S(1)} copy-done((bf16[288,128]{1,0:T(8,128)(2,1)S(1)}, bf16[288,128]{1,0:T(8,128)(2,1)}, u32[]{:S(2)}) %copy-start.5) | copy-done | bytes 73752
  7.6 0.0 copy-start.6
  7.6 0.9 %copy-done.6 = bf16[288,128]{1,0:T(8,128)(2,1)S(1)} copy-done((bf16[288,128]{1,0:T(8,128)(2,1)S(1)}, bf16[288,128]{1,0:T(8,128)(2,1)}, u32[]{:S(2)}) %copy-start.6) | copy-done | bytes 73752
  8.5 0.0 copy-start.7
  8.5 0.7 copy-done.7
  9.2 0.0 copy-start.8
  9.2 0.7 copy-done.8
  9.9 62.5 %shard_map.137 = (bf16[288,896]{1,0:T(8,128)(2,1)S(1)}, bf16[256,896]{1,0:T(8,128)(2,1)S(1)}, bf16[288,128]{1,0:T(8,128)(2,1)S(1)}, f32[64,896]{1,0:T(8,128)S(1)}, f32[64,128]{1,0:T(8,128)S(1)}) custom-call(bf16[288,896]{1,0:T(8,128)(2,1)S(1)} %copy-done.1, bf16[256,896]{1,0:T(8,128)(2,1)S(1)} %copy-done.2, bf16[288,128]{1,0:T(8,128)(2,1)S(1)} %copy-done.5, ...), custom_call_target="tpu_custom_call" | custom-call | tf_op jit(solution)/shard_map/pallas_call | solution.py:308
  72.4 0.8 %copy.21 = bf16[288,896]{1,0:T(8,128)(2,1)} copy(bf16[288,896]{1,0:T(8,128)(2,1)S(1)} %get-tuple-element.20) | data formatting | bytes 1032192
  73.2 0.8 %copy.22 = bf16[256,896]{1,0:T(8,128)(2,1)} copy(bf16[256,896]{1,0:T(8,128)(2,1)S(1)} %get-tuple-element.21) | data formatting | bytes 917504
  74.0 0.6 copy.23
  74.6 0.7 copy.24
  75.3 0.6 copy.25
Async XLA Ops:
  1.3 1.5 %copy-start = (bf16[128,7168]{1,0:T(8,128)(2,1)S(1)}, bf16[128,7168]{1,0:T(8,128)(2,1)}, u32[]{:S(2)}) copy-start(bf16[128,7168]{1,0:T(8,128)(2,1)} %w_hbm.1) | copy-start | bytes 5505028
  2.8 1.0 %copy-start.1 = (bf16[288,896]{1,0:T(8,128)(2,1)S(1)}, bf16[288,896]{1,0:T(8,128)(2,1)}, u32[]{:S(2)}) copy-start(bf16[288,896]{1,0:T(8,128)(2,1)} %x_hbm.1) | copy-start | bytes 1548292
  3.8 1.0 %copy-start.2 = (bf16[256,896]{1,0:T(8,128)(2,1)S(1)}, bf16[256,896]{1,0:T(8,128)(2,1)}, u32[]{:S(2)}) copy-start(bf16[256,896]{1,0:T(8,128)(2,1)} %q_hbm.1) | copy-start | bytes 1376260
  4.8 1.0 %copy-start.3 = (bf16[256,896]{1,0:T(8,128)(2,1)S(1)}, bf16[256,896]{1,0:T(8,128)(2,1)}, u32[]{:S(2)}) copy-start(bf16[256,896]{1,0:T(8,128)(2,1)} %g_hbm.1) | copy-start | bytes 1376260
  5.9 0.9 %copy-start.4 = (bf16[896,64]{0,1:T(8,128)(2,1)S(1)}, bf16[896,64]{0,1:T(8,128)(2,1)}, u32[]{:S(2)}) copy-start(bf16[896,64]{0,1:T(8,128)(2,1)} %param.18) | copy-start | bytes 344068
  6.8 0.9 %copy-start.5 = (bf16[288,128]{1,0:T(8,128)(2,1)S(1)}, bf16[288,128]{1,0:T(8,128)(2,1)}, u32[]{:S(2)}) copy-start(bf16[288,128]{1,0:T(8,128)(2,1)} %k_hbm.1) | copy-start | bytes 221188
  7.6 0.9 %copy-start.6 = (bf16[288,128]{1,0:T(8,128)(2,1)S(1)}, bf16[288,128]{1,0:T(8,128)(2,1)}, u32[]{:S(2)}) copy-start(bf16[288,128]{1,0:T(8,128)(2,1)} %v_hbm.1) | copy-start | bytes 221188
  8.5 0.7 copy-start.7
  9.2 0.7 copy-start.8

commit v2 on v1

--- a/solution.py
+++ b/solution.py
@@ -30,6 +30,8 @@
 RB = 128
 SEEN = (PROMPT + RB, CTX)
 
+VMEM_LIMIT = 60 * 1024 * 1024
+
 NT = (((1,), (1,)), ((), ()))
 
 
@@ -48,14 +50,15 @@
 
 
 def kernel(
-    x_hbm, q_hbm, k_hbm, v_hbm, g_hbm, mask_ref, length_ref, w_hbm, at_hbm, b_hbm,
-    lig_ref, qg_ref, kg_ref, dfg_ref, ufg_ref,
-    x_ref, q_ref, k_ref, v_ref, g_ref, at_ref,
+    x_hbm, q_hbm, k_hbm, v_hbm, g_hbm, mask_hbm, length_hbm, w_hbm, at_hbm, b_hbm,
+    lig_hbm, qg_hbm, kg_hbm, dfg_hbm, ufg_hbm,
+    x_ref, q_ref, k_ref, v_ref, g_ref, at_ref, mask_ref, length_ref,
     wfull, bfull, vgfull,
     p0, p1, pb0, pb1,
     dpart, dpieces, dfull,
     rs_src, rs_dst, bc_buf, ag_buf,
-    load_sem, w1_send, w1_recv, wz_send, wz_recv, wx_send, wx_recv, wc_send, wc_recv,
+    lig_ref, qg_ref, kg_ref, dfg_ref, ufg_ref,
+    load_sem, store_sem, w1_send, w1_recv, wz_send, wz_recv, wx_send, wx_recv, wc_send, wc_recv,
     b_send, b_recv, d1_send, d1_recv, d2_send, d2_recv, vg_send, vg_recv,
     rs_send, rs_recv, bc_send, bc_recv, ag_send, ag_recv,
 ):
@@ -89,6 +92,12 @@
         )
 
     pending = []
+    stores = [
+        pltpu.make_async_copy(src, dst, store_sem.at[i])
+        for i, (src, dst) in enumerate(
+            [(lig_ref, lig_hbm), (qg_ref, qg_hbm), (kg_ref, kg_hbm), (dfg_ref, dfg_hbm), (ufg_ref, ufg_hbm)]
+        )
+    ]
 
     def fan_out(src, dst, send, recv, devices):
         for k, device in enumerate(devices):
@@ -122,13 +131,15 @@
                 (g_hbm, g_ref),
                 (v_hbm, v_ref),
                 (b_hbm, bfull.at[y]),
+                (mask_hbm, mask_ref),
+                (length_hbm, length_ref),
             ]
         )
     ]
     for load in loads:
         load.start()
-    load_x, load_a, load_k, load_q, load_g, load_v, load_b = loads
-    w_own = pltpu.make_async_copy(w_hbm.at[w_rows, w_cols(y)], wfull.at[w_y, z], load_sem.at[7])
+    load_x, load_a, load_k, load_q, load_g, load_v, load_b, load_mask, load_length = loads
+    w_own = pltpu.make_async_copy(w_hbm.at[w_rows, w_cols(y)], wfull.at[w_y, z], load_sem.at[9])
 
     @pl.when(y == w_y)
     def _():
@@ -153,6 +164,8 @@
 
     load_k.wait()
     load_q.wait()
+    load_mask.wait()
+    load_length.wait()
     limit = PROMPT - 1 + length_ref[0]
     probs = (p0, p1)
     probs_low = (pb0, pb1)
@@ -223,6 +236,9 @@
             lanes = slice(h * HD, (h + 1) * HD)
             qg_ref[b * RB : (b + 1) * RB, lanes] = qg_t[:, lanes].T.astype(BF16)
 
+    stores[1].start()
+    stores[2].start()
+
     landed(lambda k: dfull.at[y_from[k]], d2_send, d2_recv, y_dev)
     rs_src[NZ - 1] = dot(dfull[...].reshape(RANK, CTX).astype(BF16), vgfull[y]).astype(BF16)
 
@@ -271,15 +287,20 @@
     fan_out(lambda k: ag_buf.at[z], ag_buf.at[z], ag_send, ag_recv, z_dev)
 
     input_gradient(512, 896)
+    stores[0].start()
 
     landed(lambda k: ag_buf.at[z_from[k]], ag_send, ag_recv, z_dev)
     for j in range(NZ - 1):
         dfg_ref[:, j * 128 : (j + 1) * 128] = adapter_scale * ag_buf[j].astype(F32)
     ufg_ref[...] = adapter_scale * ag_buf[NZ - 1].astype(F32)
+    stores[3].start()
+    stores[4].start()
 
     for copy in pending:
         copy.wait_send()
     to_sibling.wait_send()
+    for store in stores:
+        store.wait()
 
     @pl.when(y == w_y)
     def _():
@@ -287,6 +308,15 @@
             remote(
                 w_hbm.at[w_rows, w_cols(y_to[k])], wfull.at[w_y, z], w1_send.at[k], w1_recv, y_dev[k]
             ).wait_send()
+
+
+def hand_on(*refs):
+    sems = refs[10]
+    copies = [pltpu.make_async_copy(refs[i], refs[5 + i], sems.at[i]) for i in range(5)]
+    for copy in copies:
+        copy.start()
+    for copy in copies:
+        copy.wait()
 
 
 def per_device(
@@ -301,11 +331,9 @@
     adapter_down_factor,
     adapter_up_factor,
 ):
-    hbm = pl.BlockSpec(memory_space=pl.ANY)
-    vmem = pl.BlockSpec(memory_space=pltpu.VMEM)
-    smem = pl.BlockSpec(memory_space=pltpu.SMEM)
+    hbm = pl.BlockSpec(memory_space=pltpu.HBM)
     dma = pltpu.SemaphoreType.DMA
-    lig, qg, kg, dfg_t, ufg = pl.pallas_call(
+    outs = pl.pallas_call(
         kernel,
         out_shape=(
             jax.ShapeDtypeStruct((CTX, FEATS), BF16),
@@ -314,8 +342,8 @@
             jax.ShapeDtypeStruct((RANK, FEATS), F32),
             jax.ShapeDtypeStruct((RANK, HD), F32),
         ),
-        in_specs=[hbm, hbm, hbm, hbm, hbm, vmem, smem, hbm, hbm, hbm],
-        out_specs=(vmem,) * 5,
+        in_specs=[hbm] * 10,
+        out_specs=(hbm,) * 5,
         scratch_shapes=[
             pltpu.VMEM((CTX, FEATS), BF16),
             pltpu.VMEM((RESP, FEATS), BF16),
@@ -323,6 +351,8 @@
             pltpu.VMEM((CTX, HD), BF16),
             pltpu.VMEM((RESP, FEATS), BF16),
             pltpu.VMEM((RANK, FEATS), BF16),
+            pltpu.VMEM((1, RESP), jnp.int32),
+            pltpu.SMEM((1,), jnp.int32),
             pltpu.VMEM((NY, NZ, ROWS, FEATS), BF16),
             pltpu.VMEM((NY, RANK, HD), BF16),
             pltpu.VMEM((NY, CTX, HD), BF16),
@@ -337,7 +367,13 @@
             pltpu.VMEM((NZ, RANK, HD), BF16),
             pltpu.VMEM((NX * NC, RANK, HD), BF16),
             pltpu.VMEM((NZ, RANK, HD), BF16),
-            dma((8,)),
+            pltpu.VMEM((CTX, FEATS), BF16),
+            pltpu.VMEM((RESP, FEATS), BF16),
+            pltpu.VMEM((CTX, HD), BF16),
+            pltpu.VMEM((RANK, FEATS), F32),
+            pltpu.VMEM((RANK, HD), F32),
+            dma((10,)),
+            dma((5,)),
             dma((NY - 1,)),
             dma,
             dma((NZ - 1,)),
@@ -362,7 +398,7 @@
             dma((NZ - 1,)),
         ],
         compiler_params=pltpu.CompilerParams(
-            collective_id=0, has_side_effects=True, vmem_limit_bytes=40 * 1024 * 1024
+            collective_id=0, has_side_effects=True, vmem_limit_bytes=VMEM_LIMIT
         ),
     )(
         normed_layer_input,
@@ -376,6 +412,14 @@
         adapter_down_factor.T,
         adapter_up_factor,
     )
+    lig, qg, kg, dfg_t, ufg = pl.pallas_call(
+        hand_on,
+        out_shape=[jax.ShapeDtypeStruct(out.shape, out.dtype) for out in outs],
+        in_specs=[pl.BlockSpec(memory_space=pl.ANY)] * 5,
+        out_specs=[hbm] * 5,
+        scratch_shapes=[dma((5,))],
+        compiler_params=pltpu.CompilerParams(vmem_limit_bytes=VMEM_LIMIT),
+    )(*outs)
     return (lig, qg, kg, dfg_t.T, ufg)
 
 

time: 76.4 us -> 106 us (1.39)
  Pallas kernels: 62.5 us -> 104 us
  local copies, waits for them, and re-layouts: 12.1 us -> 0 us
    pallas_call x0 -> x1, Pallas kernels: none -> 40.9 us  [per_device(): pl.pallas_call(hand_on, out_shape=[jax.ShapeDtypeStruct(out.shape, out.dt...]
    unnamed x23 -> x0, local copies, waits for them, and re-layouts: 12.1 us -> none
    pallas_call x1, Pallas kernels: 62.5 us -> 63.6 us  [per_device(): pl.pallas_call(kernel, out_shape=(jax.ShapeDtypeStruct((CTX, FEATS), BF16...]
where the time goes in v2:
time: 106 us
  Pallas kernels  104 us (98%)
  between operations  1.29 us (1%)
    pallas_call x1, Pallas kernels, per_device(): pl.pallas_call(kernel, out_shape=(jax.ShapeDtypeStruct((CTX, FEATS), BF16...  63.6 us
    pallas_call x1, Pallas kernels, per_device(): pl.pallas_call(hand_on, out_shape=[jax.ShapeDtypeStruct(out.shape, out.dt...  40.9 us

profile of v2, /device:TPU:1, one launch (start us, length us, event | category | flops | bytes accessed | tf_op | source)
XLA Modules:
  0.0 105.7 jit_solution(3508499539909099549)
XLA Ops:
  1.3 63.6 %shard_map.137 = (bf16[288,896]{1,0:T(8,128)(2,1)}, bf16[256,896]{1,0:T(8,128)(2,1)}, bf16[288,128]{1,0:T(8,128)(2,1)}, f32[64,896]{1,0:T(8,128)}, f32[64,128]{1,0:T(8,128)}) custom-call(bf16[288,896]{1,0:T(8,128)(2,1)} %x_hbm.1, bf16[256,896]{1,0:T(8,128)(2,1)} %q_hbm.1, bf16[288,128]{1,0:T(8,128)(2,1)} %k_hbm.1, bf16[288,128]{1,0:T(8,128)(2,1)} %v_hbm.1, ...), custom_call_target="tpu_custom_call" | custom-call | tf_op jit(solution)/shard_map/pallas_call | solution.py:336
  64.9 40.9 %shard_map.138 = (bf16[288,896]{1,0:T(8,128)(2,1)}, bf16[256,896]{1,0:T(8,128)(2,1)}, bf16[288,128]{1,0:T(8,128)(2,1)}, f32[64,896]{1,0:T(8,128)}, f32[64,128]{1,0:T(8,128)}) custom-call(bf16[288,896]{1,0:T(8,128)(2,1)} %get-tuple-element.15.refs_0_, bf16[256,896]{1,0:T(8,128)(2,1)} %get-tuple-element.16.refs_1_, ...), custom_call_target="tpu_custom_call" | custom-call | tf_op jit(solution)/shard_map/pallas_call | solution.py:415

commit v3 on v2

--- a/solution.py
+++ b/solution.py
@@ -25,7 +25,10 @@
 adapter_scale = 2.0
 
 NX, NZ, NC, NY = 4, 8, 2, 8
+HALF = CTX // 2
 ROWS = 16
+
+FAR_FIRST = (4, 3, 5, 2, 6, 1, 7)
 
 RB = 128
 SEEN = (PROMPT + RB, CTX)
@@ -51,15 +54,15 @@
 
 def kernel(
     x_hbm, q_hbm, k_hbm, v_hbm, g_hbm, mask_hbm, length_hbm, w_hbm, at_hbm, b_hbm,
-    lig_hbm, qg_hbm, kg_hbm, dfg_hbm, ufg_hbm,
+    lig_hbm, qg_hbm, kg_hbm, sums_hbm,
     x_ref, q_ref, k_ref, v_ref, g_ref, at_ref, mask_ref, length_ref,
-    wfull, bfull, vgfull,
+    b_ref, wfull, vgfull,
     p0, p1, pb0, pb1,
-    dpart, dpieces, dfull,
+    downs, ups,
     rs_src, rs_dst, bc_buf, ag_buf,
-    lig_ref, qg_ref, kg_ref, dfg_ref, ufg_ref,
+    lig_ref, qg_ref, kg_ref,
     load_sem, store_sem, w1_send, w1_recv, wz_send, wz_recv, wx_send, wx_recv, wc_send, wc_recv,
-    b_send, b_recv, d1_send, d1_recv, d2_send, d2_recv, vg_send, vg_recv,
+    down_send, down_recv, up_send, up_recv, vg_send, vg_recv,
     rs_send, rs_recv, bc_send, bc_recv, ag_send, ag_recv,
 ):
     dp = lax.axis_index("dp")
@@ -71,13 +74,13 @@
     def at(px, pz, pc, py):
         return {"dp": (px * NZ + pz) * NC + pc, "tp": py}
 
-    y_to = [(y + k) % NY for k in range(1, NY)]
-    y_from = [(y + NY - k) % NY for k in range(1, NY)]
-    z_to = [(z + k) % NZ for k in range(1, NZ)]
-    z_from = [(z + NZ - k) % NZ for k in range(1, NZ)]
-    x_to = [(x + k) % NX for k in range(1, NX)]
-    x_from = [(x + NX - k) % NX for k in range(1, NX)]
-    xc_steps = [(i, j) for i in range(NX) for j in range(NC) if i or j]
+    y_to = [(y + k) % NY for k in FAR_FIRST]
+    y_from = [(y + NY - k) % NY for k in FAR_FIRST]
+    z_to = [(z + k) % NZ for k in FAR_FIRST]
+    z_from = [(z + NZ - k) % NZ for k in FAR_FIRST]
+    x_to = [(x + k) % NX for k in (2, 1, 3)]
+    x_from = [(x + NX - k) % NX for k in (2, 1, 3)]
+    xc_steps = [(i, j) for i in (2, 1, 3, 0) for j in (1, 0) if i or j]
     xc_to = [((x + i) % NX, (c + j) % NC) for i, j in xc_steps]
     xc_from = [((x + NX - i) % NX, (c + NC - j) % NC) for i, j in xc_steps]
     y_dev = [at(x, z, c, j) for j in y_to]
@@ -95,7 +98,7 @@
     stores = [
         pltpu.make_async_copy(src, dst, store_sem.at[i])
         for i, (src, dst) in enumerate(
-            [(lig_ref, lig_hbm), (qg_ref, qg_hbm), (kg_ref, kg_hbm), (dfg_ref, dfg_hbm), (ufg_ref, ufg_hbm)]
+            [(lig_ref, lig_hbm), (qg_ref, qg_hbm), (kg_ref, kg_hbm), (ag_buf, sums_hbm)]
         )
     ]
 
@@ -130,7 +133,7 @@
                 (q_hbm, q_ref),
                 (g_hbm, g_ref),
                 (v_hbm, v_ref),
-                (b_hbm, bfull.at[y]),
+                (b_hbm, b_ref),
                 (mask_hbm, mask_ref),
                 (length_hbm, length_ref),
             ]
@@ -145,10 +148,28 @@
     def _():
         w_own.start()
 
+    def first(factor):
+        return jnp.concatenate([factor, jnp.zeros_like(factor)], axis=0)
+
+    def second(factor):
+        return jnp.concatenate([jnp.zeros_like(factor), factor], axis=0)
+
+    def rank_rows(rows, factor):
+        return dot_nt(rows[:HALF], first(factor)) + dot_nt(rows[HALF:], second(factor))
+
+    def over_tokens(pairs, rows):
+        pairs_t = pairs.T.astype(BF16)
+        return dot(pairs_t, rows[:HALF])[:RANK] + dot(pairs_t, rows[HALF:])[RANK:]
+
+    def sum_of(parts):
+        total = parts[0].astype(F32)
+        for j in range(1, parts.shape[0]):
+            total = total + parts[j].astype(F32)
+        return total
+
     load_x.wait()
     load_a.wait()
-    dpart[...] = dot_nt(at_ref[...], x_ref[...]).reshape(dpart.shape)
-    load_b.wait()
+    downs[y] = rank_rows(x_ref, at_ref[...]).astype(BF16)
 
     pl.semaphore_wait(barrier, len(everyone))
 
@@ -159,8 +180,7 @@
                 w_hbm.at[w_rows, w_cols(y_to[k])], wfull.at[w_y, z], w1_send.at[k], w1_recv, y_dev[k]
             ).start()
 
-    fan_out(lambda k: dpart.at[y_to[k]], dpieces.at[y], d1_send, d1_recv, y_dev)
-    fan_out(lambda k: bfull.at[y], bfull.at[y], b_send, b_recv, y_dev)
+    fan_out(lambda k: downs.at[y], downs.at[y], down_send, down_recv, y_dev)
 
     load_k.wait()
     load_q.wait()
@@ -188,33 +208,27 @@
     for h in range(HEADS):
         for b in range(2):
             weigh(b, h)
-        if h == 1:
-            @pl.when(y == w_y)
-            def _():
-                w_own.wait()
-
-            @pl.when(y != w_y)
-            def _():
-                remote(wfull.at[w_y, z], wfull.at[w_y, z], w1_send.at[0], w1_recv, y_dev[0]).wait_recv()
-
-            fan_out(lambda k: wfull.at[w_y, z], wfull.at[w_y, z], wz_send, wz_recv, z_dev)
-        if h == 3:
-            landed(lambda k: dpieces.at[y_from[k]], d1_send, d1_recv, y_dev)
-            total = dpart[y]
-            for k in range(NY - 1):
-                total = total + dpieces[y_from[k]]
-            dfull[y] = total
-            fan_out(lambda k: dfull.at[y], dfull.at[y], d2_send, d2_recv, y_dev)
-        if h == 5:
-            landed(lambda k: wfull.at[w_y, z_from[k]], wz_send, wz_recv, z_dev)
-            fan_out(lambda k: wfull.at[w_y], wfull.at[w_y], wx_send, wx_recv, x_dev)
 
     load_g.wait()
     early = dot(pb0[...], rows_of_heads(g_ref, 0))
     late = dot(pb1[...], rows_of_heads(g_ref, 1))
     vgfull[y, : SEEN[0], :] = (early + late[: SEEN[0]]).astype(BF16)
     vgfull[y, SEEN[0] :, :] = late[SEEN[0] :].astype(BF16)
+    load_b.wait()
+    own_values = vgfull[y]
+    ups[y] = rank_rows(own_values, b_ref[...]).astype(BF16)
+    fan_out(lambda k: ups.at[y], ups.at[y], up_send, up_recv, y_dev)
     fan_out(lambda k: vgfull.at[y], vgfull.at[y], vg_send, vg_recv, y_dev)
+
+    @pl.when(y == w_y)
+    def _():
+        w_own.wait()
+
+    @pl.when(y != w_y)
+    def _():
+        remote(wfull.at[w_y, z], wfull.at[w_y, z], w1_send.at[0], w1_recv, y_dev[0]).wait_recv()
+
+    fan_out(lambda k: wfull.at[w_y, z], wfull.at[w_y, z], wz_send, wz_recv, z_dev)
 
     load_v.wait()
     for h in range(HEADS):
@@ -239,36 +253,18 @@
     stores[1].start()
     stores[2].start()
 
-    landed(lambda k: dfull.at[y_from[k]], d2_send, d2_recv, y_dev)
-    rs_src[NZ - 1] = dot(dfull[...].reshape(RANK, CTX).astype(BF16), vgfull[y]).astype(BF16)
-
-    landed(lambda k: wfull.at[4 * c + x_from[k]], wx_send, wx_recv, x_dev)
-    half = pl.ds(4 * c, 4)
-    other = pl.ds(4 * (1 - c), 4)
-    to_sibling = remote(wfull.at[half], wfull.at[half], wc_send.at[0], wc_recv.at[0], sibling)
-    to_sibling.start()
-
-    landed(lambda k: bfull.at[y_from[k]], b_send, b_recv, y_dev)
-    landed(lambda k: vgfull.at[y_from[k]], vg_send, vg_recv, y_dev)
-    values = jnp.concatenate([vgfull[j] for j in range(NY)], axis=1)
-    ups = jnp.concatenate([bfull[j] for j in range(NY)], axis=1)
-    up_t = dot_nt(ups, values).astype(BF16)
-    dfg_t = dot(up_t, x_ref[...])
+    landed(lambda k: downs.at[y_from[k]], down_send, down_recv, y_dev)
+    rs_src[NZ - 1] = over_tokens(sum_of(downs), own_values).astype(BF16)
+    landed(lambda k: ups.at[y_from[k]], up_send, up_recv, y_dev)
+    up = sum_of(ups)
+    dfg_t = over_tokens(up, x_ref)
     for j in range(NZ - 1):
         rs_src[j] = dfg_t[:, j * 128 : (j + 1) * 128].astype(BF16)
 
     fan_out(lambda k: rs_src.at[z_to[k]], rs_dst.at[z], rs_send, rs_recv, z_dev)
 
-    up = dot_nt(values, ups).astype(BF16)
-    remote(wfull.at[other], wfull.at[other], wc_send.at[0], wc_recv.at[0], sibling).wait_recv()
-
-    def input_gradient(low, high):
-        w = wfull[:, :, :, low:high].reshape(NY * HD, high - low)
-        frozen = dot(values, w)
-        adapter = dot(up, at_ref[:, low:high])
-        lig_ref[:, low:high] = (frozen + adapter_scale * adapter).astype(BF16)
-
-    input_gradient(0, 256)
+    landed(lambda k: wfull.at[w_y, z_from[k]], wz_send, wz_recv, z_dev)
+    fan_out(lambda k: wfull.at[w_y], wfull.at[w_y], wx_send, wx_recv, x_dev)
 
     landed(lambda k: rs_dst.at[z_from[k]], rs_send, rs_recv, z_dev)
     total = rs_src[z].astype(F32)
@@ -277,24 +273,29 @@
     bc_buf[x * NC + c] = total.astype(BF16)
     fan_out(lambda k: bc_buf.at[x * NC + c], bc_buf.at[x * NC + c], bc_send, bc_recv, xc_dev)
 
-    input_gradient(256, 512)
+    landed(lambda k: wfull.at[4 * c + x_from[k]], wx_send, wx_recv, x_dev)
+    half = pl.ds(4 * c, 4)
+    other = pl.ds(4 * (1 - c), 4)
+    to_sibling = remote(wfull.at[half], wfull.at[half], wc_send.at[0], wc_recv.at[0], sibling)
+    to_sibling.start()
 
     landed(lambda k: bc_buf.at[xc_from[k][0] * NC + xc_from[k][1]], bc_send, bc_recv, xc_dev)
-    total = bc_buf[0].astype(F32)
-    for j in range(1, NX * NC):
-        total = total + bc_buf[j].astype(F32)
-    ag_buf[z] = total.astype(BF16)
+    ag_buf[z] = sum_of(bc_buf).astype(BF16)
     fan_out(lambda k: ag_buf.at[z], ag_buf.at[z], ag_send, ag_recv, z_dev)
 
-    input_gradient(512, 896)
+    landed(lambda k: vgfull.at[y_from[k]], vg_send, vg_recv, y_dev)
+    remote(wfull.at[other], wfull.at[other], wc_send.at[0], wc_recv.at[0], sibling).wait_recv()
+    values = jnp.concatenate([vgfull[j] for j in range(NY)], axis=1)
+    up = up.astype(BF16)
+    for low, high in ((0, 256), (256, 512), (512, 768), (768, 896)):
+        frozen = dot(values, wfull[:, :, :, low:high].reshape(NY * HD, high - low))
+        down = at_ref[:, low:high]
+        for rows, factor in ((slice(0, HALF), first(down)), (slice(HALF, CTX), second(down))):
+            lig_ref[rows, low:high] = (frozen[rows] + adapter_scale * dot(up, factor)).astype(BF16)
     stores[0].start()
 
     landed(lambda k: ag_buf.at[z_from[k]], ag_send, ag_recv, z_dev)
-    for j in range(NZ - 1):
-        dfg_ref[:, j * 128 : (j + 1) * 128] = adapter_scale * ag_buf[j].astype(F32)
-    ufg_ref[...] = adapter_scale * ag_buf[NZ - 1].astype(F32)
     stores[3].start()
-    stores[4].start()
 
     for copy in pending:
         copy.wait_send()
@@ -310,12 +311,31 @@
             ).wait_send()
 
 
-def hand_on(*refs):
-    sems = refs[10]
-    copies = [pltpu.make_async_copy(refs[i], refs[5 + i], sems.at[i]) for i in range(5)]
-    for copy in copies:
+def hand_on(
+    lig_hbm, qg_hbm, kg_hbm, sums_hbm,
+    lig_out, qg_out, kg_out, dfg_out, ufg_out,
+    lig, qg, kg, sums, dfg, ufg, sems,
+):
+    ins = [
+        pltpu.make_async_copy(src, via, sems.at[i])
+        for i, (src, via) in enumerate([(sums_hbm, sums), (lig_hbm, lig), (qg_hbm, qg), (kg_hbm, kg)])
+    ]
+    outs = [
+        pltpu.make_async_copy(via, dst, sems.at[4 + i])
+        for i, (via, dst) in enumerate([(lig, lig_out), (qg, qg_out), (kg, kg_out), (dfg, dfg_out), (ufg, ufg_out)])
+    ]
+    for copy in ins:
         copy.start()
-    for copy in copies:
+    for i in range(3):
+        ins[i + 1].wait()
+        outs[i].start()
+    ins[0].wait()
+    for j in range(NZ - 1):
+        dfg[:, j * 128 : (j + 1) * 128] = adapter_scale * sums[j].astype(F32)
+    outs[3].start()
+    ufg[...] = adapter_scale * sums[NZ - 1].astype(F32)
+    outs[4].start()
+    for copy in outs:
         copy.wait()
 
 
@@ -339,11 +359,10 @@
             jax.ShapeDtypeStruct((CTX, FEATS), BF16),
             jax.ShapeDtypeStruct((RESP, FEATS), BF16),
             jax.ShapeDtypeStruct((CTX, HD), BF16),
-            jax.ShapeDtypeStruct((RANK, FEATS), F32),
-            jax.ShapeDtypeStruct((RANK, HD), F32),
+            jax.ShapeDtypeStruct((NZ, RANK, HD), BF16),
         ),
         in_specs=[hbm] * 10,
-        out_specs=(hbm,) * 5,
+        out_specs=(hbm,) * 4,
         scratch_shapes=[
             pltpu.VMEM((CTX, FEATS), BF16),
             pltpu.VMEM((RESP, FEATS), BF16),
@@ -353,16 +372,15 @@
             pltpu.VMEM((RANK, FEATS), BF16),
             pltpu.VMEM((1, RESP), jnp.int32),
             pltpu.SMEM((1,), jnp.int32),
+            pltpu.VMEM((RANK, HD), BF16),
             pltpu.VMEM((NY, NZ, ROWS, FEATS), BF16),
-            pltpu.VMEM((NY, RANK, HD), BF16),
             pltpu.VMEM((NY, CTX, HD), BF16),
             pltpu.VMEM((SEEN[0], FEATS), F32),
             pltpu.VMEM((SEEN[1], FEATS), F32),
             pltpu.VMEM((SEEN[0], FEATS), BF16),
             pltpu.VMEM((SEEN[1], FEATS), BF16),
-            pltpu.VMEM((NY, RANK // NY, CTX), F32),
-            pltpu.VMEM((NY, RANK // NY, CTX), F32),
-            pltpu.VMEM((NY, RANK // NY, CTX), F32),
+            pltpu.VMEM((NY, HALF, HD), BF16),
+            pltpu.VMEM((NY, HALF, HD), BF16),
             pltpu.VMEM((NZ, RANK, HD), BF16),
             pltpu.VMEM((NZ, RANK, HD), BF16),
             pltpu.VMEM((NX * NC, RANK, HD), BF16),
@@ -370,10 +388,8 @@
             pltpu.VMEM((CTX, FEATS), BF16),
             pltpu.VMEM((RESP, FEATS), BF16),
             pltpu.VMEM((CTX, HD), BF16),
-            pltpu.VMEM((RANK, FEATS), F32),
-            pltpu.VMEM((RANK, HD), F32),
             dma((10,)),
-            dma((5,)),
+            dma((4,)),
             dma((NY - 1,)),
             dma,
             dma((NZ - 1,)),
@@ -382,8 +398,6 @@
             dma((NX - 1,)),
             dma((1,)),
             dma((1,)),
-            dma((NY - 1,)),
-            dma((NY - 1,)),
             dma((NY - 1,)),
             dma((NY - 1,)),
             dma((NY - 1,)),
@@ -414,10 +428,24 @@
     )
     lig, qg, kg, dfg_t, ufg = pl.pallas_call(
         hand_on,
-        out_shape=[jax.ShapeDtypeStruct(out.shape, out.dtype) for out in outs],
-        in_specs=[pl.BlockSpec(memory_space=pl.ANY)] * 5,
-        out_specs=[hbm] * 5,
-        scratch_shapes=[dma((5,))],
+        out_shape=(
+            jax.ShapeDtypeStruct((CTX, FEATS), BF16),
+            jax.ShapeDtypeStruct((RESP, FEATS), BF16),
+            jax.ShapeDtypeStruct((CTX, HD), BF16),
+            jax.ShapeDtypeStruct((RANK, FEATS), F32),
+            jax.ShapeDtypeStruct((RANK, HD), F32),
+        ),
+        in_specs=[hbm] * 4,
+        out_specs=(hbm,) * 5,
+        scratch_shapes=[
+            pltpu.VMEM((CTX, FEATS), BF16),
+            pltpu.VMEM((RESP, FEATS), BF16),
+            pltpu.VMEM((CTX, HD), BF16),
+            pltpu.VMEM((NZ, RANK, HD), BF16),
+            pltpu.VMEM((RANK, FEATS), F32),
+            pltpu.VMEM((RANK, HD), F32),
+            dma((9,)),
+        ],
         compiler_params=pltpu.CompilerParams(vmem_limit_bytes=VMEM_LIMIT),
     )(*outs)
     return (lig, qg, kg, dfg_t.T, ufg)

time: 106 us -> 58.3 us (0.55)
  the two profiles are of different devices: /device:TPU:1 before, /device:TPU:24 now
where the time goes in v3:
time: 58.3 us; the launch traced here: 58.1 us
  Pallas kernels  56.8 us (97%)
  between operations  1.29 us (2%)
    pallas_call x1, Pallas kernels, per_device(): pl.pallas_call(kernel, out_shape=(jax.ShapeDtypeStruct((CTX, FEATS), BF16...  54.6 us
    pallas_call x1, Pallas kernels, per_device(): pl.pallas_call(hand_on, out_shape=(jax.ShapeDtypeStruct((CTX, FEATS), BF1...  2.23 us

profile of v3, /device:TPU:24, one launch (start us, length us, event | category | flops | bytes accessed | tf_op | source)
XLA Modules:
  0.0 58.1 jit_solution(13488453104856917102)
XLA Ops:
  1.3 54.6 %shard_map.137 = (bf16[288,896]{1,0:T(8,128)(2,1)}, bf16[256,896]{1,0:T(8,128)(2,1)}, bf16[288,128]{1,0:T(8,128)(2,1)}, bf16[8,64,128]{2,1,0:T(8,128)(2,1)}) custom-call(bf16[288,896]{1,0:T(8,128)(2,1)} %x_hbm.1, bf16[256,896]{1,0:T(8,128)(2,1)} %q_hbm.1, bf16[288,128]{1,0:T(8,128)(2,1)} %k_hbm.1, bf16[288,128]{1,0:T(8,128)(2,1)} %v_hbm.1, ...), custom_call_target="tpu_custom_call" | custom-call | tf_op jit(solution)/shard_map/pallas_call | solution.py:356
  55.9 2.2 %shard_map.138 = (bf16[288,896]{1,0:T(8,128)(2,1)}, bf16[256,896]{1,0:T(8,128)(2,1)}, bf16[288,128]{1,0:T(8,128)(2,1)}, f32[64,896]{1,0:T(8,128)}, f32[64,128]{1,0:T(8,128)}) custom-call(bf16[288,896]{1,0:T(8,128)(2,1)} %get-tuple-element.14.lig_hbm, bf16[256,896]{1,0:T(8,128)(2,1)} %get-tuple-element.15.qg_hbm, bf16[288,128]{1,0:T(8,128)(2,1)} %get-tuple-element.16.kg_hbm, ...), custom_call_target="tpu_custom_call" | custom-call | tf_op jit(solution)/shard_map/pallas_call | solution.py:429

commit v4 on v3

--- a/solution.py
+++ b/solution.py
@@ -58,11 +58,11 @@
     x_ref, q_ref, k_ref, v_ref, g_ref, at_ref, mask_ref, length_ref,
     b_ref, wfull, vgfull,
     p0, p1, pb0, pb1,
-    downs, ups,
-    rs_src, rs_dst, bc_buf, ag_buf,
+    down_out, down_in, downs, ups,
+    rs_src, rs_dst, bc_buf, total_ref,
     lig_ref, qg_ref, kg_ref,
     load_sem, store_sem, w1_send, w1_recv, wz_send, wz_recv, wx_send, wx_recv, wc_send, wc_recv,
-    down_send, down_recv, up_send, up_recv, vg_send, vg_recv,
+    d1_send, d1_recv, d2_send, d2_recv, up_send, up_recv, vg_send, vg_recv,
     rs_send, rs_recv, bc_send, bc_recv, ag_send, ag_recv,
 ):
     dp = lax.axis_index("dp")
@@ -98,7 +98,7 @@
     stores = [
         pltpu.make_async_copy(src, dst, store_sem.at[i])
         for i, (src, dst) in enumerate(
-            [(lig_ref, lig_hbm), (qg_ref, qg_hbm), (kg_ref, kg_hbm), (ag_buf, sums_hbm)]
+            [(lig_ref, lig_hbm), (qg_ref, qg_hbm), (kg_ref, kg_hbm), (total_ref, sums_hbm.at[z])]
         )
     ]
 
@@ -169,18 +169,10 @@
 
     load_x.wait()
     load_a.wait()
-    downs[y] = rank_rows(x_ref, at_ref[...]).astype(BF16)
-
-    pl.semaphore_wait(barrier, len(everyone))
-
-    @pl.when(y == w_y)
-    def _():
-        for k in range(NY - 1):
-            remote(
-                w_hbm.at[w_rows, w_cols(y_to[k])], wfull.at[w_y, z], w1_send.at[k], w1_recv, y_dev[k]
-            ).start()
-
-    fan_out(lambda k: downs.at[y], downs.at[y], down_send, down_recv, y_dev)
+    down = rank_rows(x_ref, at_ref[...]).astype(BF16)
+    for j in range(NY):
+        down_out[j, 0] = down[j * ROWS : (j + 1) * ROWS]
+        down_out[j, 1] = down[NY * ROWS :]
 
     load_k.wait()
     load_q.wait()
@@ -217,18 +209,18 @@
     load_b.wait()
     own_values = vgfull[y]
     ups[y] = rank_rows(own_values, b_ref[...]).astype(BF16)
-    fan_out(lambda k: ups.at[y], ups.at[y], up_send, up_recv, y_dev)
-    fan_out(lambda k: vgfull.at[y], vgfull.at[y], vg_send, vg_recv, y_dev)
+
+    pl.semaphore_wait(barrier, len(everyone))
 
     @pl.when(y == w_y)
     def _():
-        w_own.wait()
-
-    @pl.when(y != w_y)
-    def _():
-        remote(wfull.at[w_y, z], wfull.at[w_y, z], w1_send.at[0], w1_recv, y_dev[0]).wait_recv()
-
-    fan_out(lambda k: wfull.at[w_y, z], wfull.at[w_y, z], wz_send, wz_recv, z_dev)
+        for k in range(NY - 1):
+            remote(
+                w_hbm.at[w_rows, w_cols(y_to[k])], wfull.at[w_y, z], w1_send.at[k], w1_recv, y_dev[k]
+            ).start()
+
+    fan_out(lambda k: down_out.at[y_to[k]], down_in.at[y], d1_send, d1_recv, y_dev)
+    fan_out(lambda k: ups.at[y], ups.at[y], up_send, up_recv, y_dev)
 
     load_v.wait()
     for h in range(HEADS):
@@ -253,18 +245,54 @@
     stores[1].start()
     stores[2].start()
 
-    landed(lambda k: downs.at[y_from[k]], down_send, down_recv, y_dev)
-    rs_src[NZ - 1] = over_tokens(sum_of(downs), own_values).astype(BF16)
+    @pl.when(y == w_y)
+    def _():
+        w_own.wait()
+
+    @pl.when(y != w_y)
+    def _():
+        remote(wfull.at[w_y, z], wfull.at[w_y, z], w1_send.at[0], w1_recv, y_dev[0]).wait_recv()
+
+    fan_out(lambda k: wfull.at[w_y, z], wfull.at[w_y, z], wz_send, wz_recv, z_dev)
+
+    landed(lambda k: down_in.at[y_from[k]], d1_send, d1_recv, y_dev)
+    piece = down_out[y].astype(F32)
+    for k in range(NY - 1):
+        piece = piece + down_in[y_from[k]].astype(F32)
+    downs[y] = piece[0].astype(BF16)
+    fan_out(lambda k: downs.at[y], downs.at[y], d2_send, d2_recv, y_dev)
+
+    def send_core(k, block):
+        return remote(wfull.at[block], wfull.at[block], wc_send.at[k], wc_recv.at[k], sibling)
+
+    def send_rs(k):
+        return remote(rs_src.at[z_to[k]], rs_dst.at[z], rs_send.at[k], rs_recv.at[k], z_dev[k])
+
+    landed(lambda k: wfull.at[w_y, z_from[k]], wz_send, wz_recv, z_dev)
+    fan_out(lambda k: wfull.at[w_y], wfull.at[w_y], wx_send, wx_recv, x_dev)
+    send_core(0, w_y).start()
+
     landed(lambda k: ups.at[y_from[k]], up_send, up_recv, y_dev)
+    fan_out(lambda k: vgfull.at[y], vgfull.at[y], vg_send, vg_recv, y_dev)
     up = sum_of(ups)
     dfg_t = over_tokens(up, x_ref)
     for j in range(NZ - 1):
         rs_src[j] = dfg_t[:, j * 128 : (j + 1) * 128].astype(BF16)
-
-    fan_out(lambda k: rs_src.at[z_to[k]], rs_dst.at[z], rs_send, rs_recv, z_dev)
-
-    landed(lambda k: wfull.at[w_y, z_from[k]], wz_send, wz_recv, z_dev)
-    fan_out(lambda k: wfull.at[w_y], wfull.at[w_y], wx_send, wx_recv, x_dev)
+    for k in range(NZ - 1):
+
+        @pl.when(z_to[k] < NZ - 1)
+        def _():
+            send_rs(k).start()
+
+    landed(lambda k: downs.at[y_from[k]], d2_send, d2_recv, y_dev)
+    down = jnp.concatenate([downs[...].reshape(NY * ROWS, HD).astype(F32), piece[1]], axis=0)
+    rs_src[NZ - 1] = over_tokens(down, own_values).astype(BF16)
+
+    for k in range(NZ - 1):
+
+        @pl.when(z_to[k] == NZ - 1)
+        def _():
+            send_rs(k).start()
 
     landed(lambda k: rs_dst.at[z_from[k]], rs_send, rs_recv, z_dev)
     total = rs_src[z].astype(F32)
@@ -273,18 +301,18 @@
     bc_buf[x * NC + c] = total.astype(BF16)
     fan_out(lambda k: bc_buf.at[x * NC + c], bc_buf.at[x * NC + c], bc_send, bc_recv, xc_dev)
 
-    landed(lambda k: wfull.at[4 * c + x_from[k]], wx_send, wx_recv, x_dev)
-    half = pl.ds(4 * c, 4)
-    other = pl.ds(4 * (1 - c), 4)
-    to_sibling = remote(wfull.at[half], wfull.at[half], wc_send.at[0], wc_recv.at[0], sibling)
-    to_sibling.start()
-
     landed(lambda k: bc_buf.at[xc_from[k][0] * NC + xc_from[k][1]], bc_send, bc_recv, xc_dev)
-    ag_buf[z] = sum_of(bc_buf).astype(BF16)
-    fan_out(lambda k: ag_buf.at[z], ag_buf.at[z], ag_send, ag_recv, z_dev)
+    total_ref[...] = sum_of(bc_buf).astype(BF16)
+    stores[3].start()
+    fan_out(lambda k: total_ref, sums_hbm.at[z], ag_send, ag_recv, z_dev)
+    for k in range(NX - 1):
+        remote(wfull.at[4 * c + x_from[k]], wfull.at[4 * c + x_from[k]], wx_send.at[k], wx_recv.at[k], x_dev[k]).wait_recv()
+        send_core(1 + k, 4 * c + x_from[k]).start()
 
     landed(lambda k: vgfull.at[y_from[k]], vg_send, vg_recv, y_dev)
-    remote(wfull.at[other], wfull.at[other], wc_send.at[0], wc_recv.at[0], sibling).wait_recv()
+    send_core(0, 4 * (1 - c) + x).wait_recv()
+    for k in range(NX - 1):
+        send_core(1 + k, 4 * (1 - c) + x_from[k]).wait_recv()
     values = jnp.concatenate([vgfull[j] for j in range(NY)], axis=1)
     up = up.astype(BF16)
     for low, high in ((0, 256), (256, 512), (512, 768), (768, 896)):
@@ -294,12 +322,15 @@
             lig_ref[rows, low:high] = (frozen[rows] + adapter_scale * dot(up, factor)).astype(BF16)
     stores[0].start()
 
-    landed(lambda k: ag_buf.at[z_from[k]], ag_send, ag_recv, z_dev)
-    stores[3].start()
-
+    landed(lambda k: sums_hbm.at[z_from[k]], ag_send, ag_recv, z_dev)
+
+    for k in range(NZ - 1):
+        send_rs(k).wait_send()
+    send_core(0, w_y).wait_send()
+    for k in range(NX - 1):
+        send_core(1 + k, 4 * c + x_from[k]).wait_send()
     for copy in pending:
         copy.wait_send()
-    to_sibling.wait_send()
     for store in stores:
         store.wait()
 
@@ -379,12 +410,14 @@
             pltpu.VMEM((SEEN[1], FEATS), F32),
             pltpu.VMEM((SEEN[0], FEATS), BF16),
             pltpu.VMEM((SEEN[1], FEATS), BF16),
-            pltpu.VMEM((NY, HALF, HD), BF16),
+            pltpu.VMEM((NY, 2, ROWS, HD), BF16),
+            pltpu.VMEM((NY, 2, ROWS, HD), BF16),
+            pltpu.VMEM((NY, ROWS, HD), BF16),
             pltpu.VMEM((NY, HALF, HD), BF16),
             pltpu.VMEM((NZ, RANK, HD), BF16),
             pltpu.VMEM((NZ, RANK, HD), BF16),
             pltpu.VMEM((NX * NC, RANK, HD), BF16),
-            pltpu.VMEM((NZ, RANK, HD), BF16),
+            pltpu.VMEM((RANK, HD), BF16),
             pltpu.VMEM((CTX, FEATS), BF16),
             pltpu.VMEM((RESP, FEATS), BF16),
             pltpu.VMEM((CTX, HD), BF16),
@@ -396,8 +429,10 @@
             dma((NZ - 1,)),
             dma((NX - 1,)),
             dma((NX - 1,)),
-            dma((1,)),
-            dma((1,)),
+            dma((NX,)),
+            dma((NX,)),
+            dma((NY - 1,)),
+            dma((NY - 1,)),
             dma((NY - 1,)),
             dma((NY - 1,)),
             dma((NY - 1,)),

time: 58.3 us -> 50.7 us (0.87)
  the two profiles are of different devices: /device:TPU:24 before, /device:TPU:1 now
where the time goes in v4:
time: 50.7 us; the launch traced here: 50.2 us
  Pallas kernels  48.9 us (96%)
  between operations  1.29 us (3%)
    pallas_call x1, Pallas kernels, per_device(): pl.pallas_call(kernel, out_shape=(jax.ShapeDtypeStruct((CTX, FEATS), BF16...  46.7 us
    pallas_call x1, Pallas kernels, per_device(): pl.pallas_call(hand_on, out_shape=(jax.ShapeDtypeStruct((CTX, FEATS), BF1...  2.23 us

profile of v4, /device:TPU:1, one launch (start us, length us, event | category | flops | bytes accessed | tf_op | source)
XLA Modules:
  0.0 50.2 jit_solution(1248086937385146657)
XLA Ops:
  1.3 46.7 %shard_map.137 = (bf16[288,896]{1,0:T(8,128)(2,1)}, bf16[256,896]{1,0:T(8,128)(2,1)}, bf16[288,128]{1,0:T(8,128)(2,1)}, bf16[8,64,128]{2,1,0:T(8,128)(2,1)}) custom-call(bf16[288,896]{1,0:T(8,128)(2,1)} %x_hbm.1, bf16[256,896]{1,0:T(8,128)(2,1)} %q_hbm.1, bf16[288,128]{1,0:T(8,128)(2,1)} %k_hbm.1, bf16[288,128]{1,0:T(8,128)(2,1)} %v_hbm.1, ...), custom_call_target="tpu_custom_call" | custom-call | tf_op jit(solution)/shard_map/pallas_call | solution.py:387
  48.0 2.2 %shard_map.138 = (bf16[288,896]{1,0:T(8,128)(2,1)}, bf16[256,896]{1,0:T(8,128)(2,1)}, bf16[288,128]{1,0:T(8,128)(2,1)}, f32[64,896]{1,0:T(8,128)}, f32[64,128]{1,0:T(8,128)}) custom-call(bf16[288,896]{1,0:T(8,128)(2,1)} %get-tuple-element.14.lig_hbm, bf16[256,896]{1,0:T(8,128)(2,1)} %get-tuple-element.15.qg_hbm, bf16[288,128]{1,0:T(8,128)(2,1)} %get-tuple-element.16.kg_hbm, ...), custom_call_target="tpu_custom_call" | custom-call | tf_op jit(solution)/shard_map/pallas_call | solution.py:464

commit v5 on v4

--- a/solution.py
+++ b/solution.py
@@ -58,11 +58,11 @@
     x_ref, q_ref, k_ref, v_ref, g_ref, at_ref, mask_ref, length_ref,
     b_ref, wfull, vgfull,
     p0, p1, pb0, pb1,
-    down_out, down_in, downs, ups,
+    parts_out, parts_in, sums,
     rs_src, rs_dst, bc_buf, total_ref,
     lig_ref, qg_ref, kg_ref,
     load_sem, store_sem, w1_send, w1_recv, wz_send, wz_recv, wx_send, wx_recv, wc_send, wc_recv,
-    d1_send, d1_recv, d2_send, d2_recv, up_send, up_recv, vg_send, vg_recv,
+    d1_send, d1_recv, d2_send, d2_recv, vg_send, vg_recv,
     rs_send, rs_recv, bc_send, bc_recv, ag_send, ag_recv,
 ):
     dp = lax.axis_index("dp")
@@ -112,11 +112,6 @@
         for k, device in enumerate(devices):
             remote(dst(k), dst(k), send.at[k], recv.at[k], device).wait_recv()
 
-    barrier = pltpu.get_barrier_semaphore()
-    everyone = y_dev + z_dev + xc_dev
-    for device in everyone:
-        pl.semaphore_signal(barrier, inc=1, device_id=device, device_id_type=MESH)
-
     w_y = 4 * c + x
     w_rows = pl.ds(pl.multiple_of(z * ROWS, ROWS), ROWS)
 
@@ -127,10 +122,10 @@
         pltpu.make_async_copy(src, dst, load_sem.at[i])
         for i, (src, dst) in enumerate(
             [
+                (k_hbm, k_ref),
+                (q_hbm, q_ref),
                 (x_hbm, x_ref),
                 (at_hbm, at_ref),
-                (k_hbm, k_ref),
-                (q_hbm, q_ref),
                 (g_hbm, g_ref),
                 (v_hbm, v_ref),
                 (b_hbm, b_ref),
@@ -141,7 +136,12 @@
     ]
     for load in loads:
         load.start()
-    load_x, load_a, load_k, load_q, load_g, load_v, load_b, load_mask, load_length = loads
+    barrier = pltpu.get_barrier_semaphore()
+    everyone = y_dev + z_dev + xc_dev
+    for device in everyone:
+        pl.semaphore_signal(barrier, inc=1, device_id=device, device_id_type=MESH)
+
+    load_k, load_q, load_x, load_a, load_g, load_v, load_b, load_mask, load_length = loads
     w_own = pltpu.make_async_copy(w_hbm.at[w_rows, w_cols(y)], wfull.at[w_y, z], load_sem.at[9])
 
     @pl.when(y == w_y)
@@ -166,13 +166,6 @@
         for j in range(1, parts.shape[0]):
             total = total + parts[j].astype(F32)
         return total
-
-    load_x.wait()
-    load_a.wait()
-    down = rank_rows(x_ref, at_ref[...]).astype(BF16)
-    for j in range(NY):
-        down_out[j, 0] = down[j * ROWS : (j + 1) * ROWS]
-        down_out[j, 1] = down[NY * ROWS :]
 
     load_k.wait()
     load_q.wait()
@@ -201,6 +194,15 @@
         for b in range(2):
             weigh(b, h)
 
+    def hand_out(i, rows):
+        rows = rows.astype(BF16)
+        for j in range(NY):
+            parts_out[j, i] = rows[j * ROWS : (j + 1) * ROWS]
+            parts_out[j, 2 + i] = rows[NY * ROWS :]
+
+    load_x.wait()
+    load_a.wait()
+    hand_out(0, rank_rows(x_ref, at_ref[...]))
     load_g.wait()
     early = dot(pb0[...], rows_of_heads(g_ref, 0))
     late = dot(pb1[...], rows_of_heads(g_ref, 1))
@@ -208,7 +210,7 @@
     vgfull[y, SEEN[0] :, :] = late[SEEN[0] :].astype(BF16)
     load_b.wait()
     own_values = vgfull[y]
-    ups[y] = rank_rows(own_values, b_ref[...]).astype(BF16)
+    hand_out(1, rank_rows(own_values, b_ref[...]))
 
     pl.semaphore_wait(barrier, len(everyone))
 
@@ -219,8 +221,7 @@
                 w_hbm.at[w_rows, w_cols(y_to[k])], wfull.at[w_y, z], w1_send.at[k], w1_recv, y_dev[k]
             ).start()
 
-    fan_out(lambda k: down_out.at[y_to[k]], down_in.at[y], d1_send, d1_recv, y_dev)
-    fan_out(lambda k: ups.at[y], ups.at[y], up_send, up_recv, y_dev)
+    fan_out(lambda k: parts_out.at[y_to[k]], parts_in.at[y], d1_send, d1_recv, y_dev)
 
     load_v.wait()
     for h in range(HEADS):
@@ -255,44 +256,37 @@
 
     fan_out(lambda k: wfull.at[w_y, z], wfull.at[w_y, z], wz_send, wz_recv, z_dev)
 
-    landed(lambda k: down_in.at[y_from[k]], d1_send, d1_recv, y_dev)
-    piece = down_out[y].astype(F32)
+    landed(lambda k: parts_in.at[y_from[k]], d1_send, d1_recv, y_dev)
+    total_rows = parts_out[y].astype(F32)
     for k in range(NY - 1):
-        piece = piece + down_in[y_from[k]].astype(F32)
-    downs[y] = piece[0].astype(BF16)
-    fan_out(lambda k: downs.at[y], downs.at[y], d2_send, d2_recv, y_dev)
+        total_rows = total_rows + parts_in[y_from[k]].astype(F32)
+    sums[y] = total_rows[:2].astype(BF16)
+    fan_out(lambda k: sums.at[y], sums.at[y], d2_send, d2_recv, y_dev)
+
+    def summed(i):
+        return jnp.concatenate([sums[:, i].reshape(NY * ROWS, HD).astype(F32), total_rows[2 + i]], axis=0)
+
+    def first_half(block):
+        return wfull.at[block, : NZ // 2]
+
+    def second_half(block):
+        return wfull.at[block, NZ // 2 :]
 
     def send_core(k, block):
         return remote(wfull.at[block], wfull.at[block], wc_send.at[k], wc_recv.at[k], sibling)
 
-    def send_rs(k):
-        return remote(rs_src.at[z_to[k]], rs_dst.at[z], rs_send.at[k], rs_recv.at[k], z_dev[k])
-
-    landed(lambda k: wfull.at[w_y, z_from[k]], wz_send, wz_recv, z_dev)
-    fan_out(lambda k: wfull.at[w_y], wfull.at[w_y], wx_send, wx_recv, x_dev)
-    send_core(0, w_y).start()
-
-    landed(lambda k: ups.at[y_from[k]], up_send, up_recv, y_dev)
+    landed(lambda k: sums.at[y_from[k]], d2_send, d2_recv, y_dev)
     fan_out(lambda k: vgfull.at[y], vgfull.at[y], vg_send, vg_recv, y_dev)
-    up = sum_of(ups)
+    up = summed(1)
     dfg_t = over_tokens(up, x_ref)
     for j in range(NZ - 1):
         rs_src[j] = dfg_t[:, j * 128 : (j + 1) * 128].astype(BF16)
-    for k in range(NZ - 1):
-
-        @pl.when(z_to[k] < NZ - 1)
-        def _():
-            send_rs(k).start()
-
-    landed(lambda k: downs.at[y_from[k]], d2_send, d2_recv, y_dev)
-    down = jnp.concatenate([downs[...].reshape(NY * ROWS, HD).astype(F32), piece[1]], axis=0)
-    rs_src[NZ - 1] = over_tokens(down, own_values).astype(BF16)
-
-    for k in range(NZ - 1):
-
-        @pl.when(z_to[k] == NZ - 1)
-        def _():
-            send_rs(k).start()
+    rs_src[NZ - 1] = over_tokens(summed(0), own_values).astype(BF16)
+    fan_out(lambda k: rs_src.at[z_to[k]], rs_dst.at[z], rs_send, rs_recv, z_dev)
+
+    landed(lambda k: wfull.at[w_y, z_from[k]], wz_send, wz_recv, z_dev)
+    fan_out(lambda k: first_half(w_y), first_half(w_y), wx_send.at[0], wx_recv.at[0], x_dev)
+    send_core(0, w_y).start()
 
     landed(lambda k: rs_dst.at[z_from[k]], rs_send, rs_recv, z_dev)
     total = rs_src[z].astype(F32)
@@ -300,14 +294,17 @@
         total = total + rs_dst[z_from[k]].astype(F32)
     bc_buf[x * NC + c] = total.astype(BF16)
     fan_out(lambda k: bc_buf.at[x * NC + c], bc_buf.at[x * NC + c], bc_send, bc_recv, xc_dev)
+    fan_out(lambda k: second_half(w_y), second_half(w_y), wx_send.at[1], wx_recv.at[1], x_dev)
 
     landed(lambda k: bc_buf.at[xc_from[k][0] * NC + xc_from[k][1]], bc_send, bc_recv, xc_dev)
     total_ref[...] = sum_of(bc_buf).astype(BF16)
     stores[3].start()
     fan_out(lambda k: total_ref, sums_hbm.at[z], ag_send, ag_recv, z_dev)
     for k in range(NX - 1):
-        remote(wfull.at[4 * c + x_from[k]], wfull.at[4 * c + x_from[k]], wx_send.at[k], wx_recv.at[k], x_dev[k]).wait_recv()
-        send_core(1 + k, 4 * c + x_from[k]).start()
+        block = 4 * c + x_from[k]
+        for i, half in enumerate((first_half(block), second_half(block))):
+            remote(half, half, wx_send.at[i, k], wx_recv.at[i, k], x_dev[k]).wait_recv()
+        send_core(1 + k, block).start()
 
     landed(lambda k: vgfull.at[y_from[k]], vg_send, vg_recv, y_dev)
     send_core(0, 4 * (1 - c) + x).wait_recv()
@@ -324,8 +321,6 @@
 
     landed(lambda k: sums_hbm.at[z_from[k]], ag_send, ag_recv, z_dev)
 
-    for k in range(NZ - 1):
-        send_rs(k).wait_send()
     send_core(0, w_y).wait_send()
     for k in range(NX - 1):
         send_core(1 + k, 4 * c + x_from[k]).wait_send()
@@ -345,27 +340,30 @@
 def hand_on(
     lig_hbm, qg_hbm, kg_hbm, sums_hbm,
     lig_out, qg_out, kg_out, dfg_out, ufg_out,
-    lig, qg, kg, sums, dfg, ufg, sems,
+    lig, qg, kg, sums, dfg, ufg, in_sems, out_sems,
 ):
-    ins = [
-        pltpu.make_async_copy(src, via, sems.at[i])
-        for i, (src, via) in enumerate([(sums_hbm, sums), (lig_hbm, lig), (qg_hbm, qg), (kg_hbm, kg)])
-    ]
-    outs = [
-        pltpu.make_async_copy(via, dst, sems.at[4 + i])
-        for i, (via, dst) in enumerate([(lig, lig_out), (qg, qg_out), (kg, kg_out), (dfg, dfg_out), (ufg, ufg_out)])
+    pieces = [(sums_hbm, sums, None)]
+    for src, via, dst, step in ((lig_hbm, lig, lig_out, 96), (qg_hbm, qg, qg_out, 64), (kg_hbm, kg, kg_out, CTX)):
+        for low in range(0, src.shape[0], step):
+            rows = pl.ds(low, step)
+            pieces.append((src.at[rows], via.at[rows], dst.at[rows]))
+    ins = [pltpu.make_async_copy(src, via, in_sems.at[i]) for i, (src, via, _) in enumerate(pieces)]
+    outs = [pltpu.make_async_copy(via, dst, out_sems.at[i]) for i, (_, via, dst) in enumerate(pieces[1:])]
+    outs += [
+        pltpu.make_async_copy(via, dst, out_sems.at[len(outs) + i])
+        for i, (via, dst) in enumerate([(dfg, dfg_out), (ufg, ufg_out)])
     ]
     for copy in ins:
         copy.start()
-    for i in range(3):
-        ins[i + 1].wait()
-        outs[i].start()
     ins[0].wait()
     for j in range(NZ - 1):
         dfg[:, j * 128 : (j + 1) * 128] = adapter_scale * sums[j].astype(F32)
-    outs[3].start()
     ufg[...] = adapter_scale * sums[NZ - 1].astype(F32)
-    outs[4].start()
+    outs[-2].start()
+    outs[-1].start()
+    for before, after in zip(ins[1:], outs):
+        before.wait()
+        after.start()
     for copy in outs:
         copy.wait()
 
@@ -410,10 +408,9 @@
             pltpu.VMEM((SEEN[1], FEATS), F32),
             pltpu.VMEM((SEEN[0], FEATS), BF16),
             pltpu.VMEM((SEEN[1], FEATS), BF16),
+            pltpu.VMEM((NY, 4, ROWS, HD), BF16),
+            pltpu.VMEM((NY, 4, ROWS, HD), BF16),
             pltpu.VMEM((NY, 2, ROWS, HD), BF16),
-            pltpu.VMEM((NY, 2, ROWS, HD), BF16),
-            pltpu.VMEM((NY, ROWS, HD), BF16),
-            pltpu.VMEM((NY, HALF, HD), BF16),
             pltpu.VMEM((NZ, RANK, HD), BF16),
             pltpu.VMEM((NZ, RANK, HD), BF16),
             pltpu.VMEM((NX * NC, RANK, HD), BF16),
@@ -427,12 +424,10 @@
             dma,
             dma((NZ - 1,)),
             dma((NZ - 1,)),
-            dma((NX - 1,)),
-            dma((NX - 1,)),
+            dma((2, NX - 1)),
+            dma((2, NX - 1)),
             dma((NX,)),
             dma((NX,)),
-            dma((NY - 1,)),
-            dma((NY - 1,)),
             dma((NY - 1,)),
             dma((NY - 1,)),
             dma((NY - 1,)),
@@ -480,6 +475,7 @@
             pltpu.VMEM((RANK, FEATS), F32),
             pltpu.VMEM((RANK, HD), F32),
             dma((9,)),
+            dma((10,)),
         ],
         compiler_params=pltpu.CompilerParams(vmem_limit_bytes=VMEM_LIMIT),
     )(*outs)

time: 50.7 us -> 50 us (0.986)
  no operation moved by 1% of the time
where the time goes in v5:
time: 50 us; the launch traced here: 49.8 us
  Pallas kernels  48.5 us (97%)
  between operations  1.29 us (3%)
    pallas_call x1, Pallas kernels, per_device(): pl.pallas_call(kernel, out_shape=(jax.ShapeDtypeStruct((CTX, FEATS), BF16...  46.3 us
    pallas_call x1, Pallas kernels, per_device(): pl.pallas_call(hand_on, out_shape=(jax.ShapeDtypeStruct((CTX, FEATS), BF1...  2.17 us

profile of v5, /device:TPU:1, one launch (start us, length us, event | category | flops | bytes accessed | tf_op | source)
XLA Modules:
  0.0 49.8 jit_solution(9820478359644212487)
XLA Ops:
  1.3 46.3 %shard_map.137 = (bf16[288,896]{1,0:T(8,128)(2,1)}, bf16[256,896]{1,0:T(8,128)(2,1)}, bf16[288,128]{1,0:T(8,128)(2,1)}, bf16[8,64,128]{2,1,0:T(8,128)(2,1)}) custom-call(bf16[288,896]{1,0:T(8,128)(2,1)} %x_hbm.1, bf16[256,896]{1,0:T(8,128)(2,1)} %q_hbm.1, bf16[288,128]{1,0:T(8,128)(2,1)} %k_hbm.1, bf16[288,128]{1,0:T(8,128)(2,1)} %v_hbm.1, ...), custom_call_target="tpu_custom_call" | custom-call | tf_op jit(solution)/shard_map/pallas_call | solution.py:385
  47.6 2.2 %shard_map.138 = (bf16[288,896]{1,0:T(8,128)(2,1)}, bf16[256,896]{1,0:T(8,128)(2,1)}, bf16[288,128]{1,0:T(8,128)(2,1)}, f32[64,896]{1,0:T(8,128)}, f32[64,128]{1,0:T(8,128)}) custom-call(bf16[288,896]{1,0:T(8,128)(2,1)} %get-tuple-element.14.lig_hbm, bf16[256,896]{1,0:T(8,128)(2,1)} %get-tuple-element.15.qg_hbm, bf16[288,128]{1,0:T(8,128)(2,1)} %get-tuple-element.16.kg_hbm, ...), custom_call_target="tpu_custom_call" | custom-call | tf_op jit(solution)/shard_map/pallas_call | solution.py:459

commit v6 on v5

--- a/solution.py
+++ b/solution.py
@@ -27,6 +27,8 @@
 NX, NZ, NC, NY = 4, 8, 2, 8
 HALF = CTX // 2
 ROWS = 16
+
+WEIGHT_PARTS = ((0, 512), (512, 384))
 
 FAR_FIRST = (4, 3, 5, 2, 6, 1, 7)
 
@@ -98,7 +100,8 @@
     stores = [
         pltpu.make_async_copy(src, dst, store_sem.at[i])
         for i, (src, dst) in enumerate(
-            [(lig_ref, lig_hbm), (qg_ref, qg_hbm), (kg_ref, kg_hbm), (total_ref, sums_hbm.at[z])]
+            [(qg_ref, qg_hbm), (kg_ref, kg_hbm), (total_ref, sums_hbm.at[z])]
+            + [(lig_ref.at[:, pl.ds(*cols)], lig_hbm.at[:, pl.ds(*cols)]) for cols in WEIGHT_PARTS]
         )
     ]
 
@@ -214,14 +217,14 @@
 
     pl.semaphore_wait(barrier, len(everyone))
 
+    fan_out(lambda k: parts_out.at[y_to[k]], parts_in.at[y], d1_send, d1_recv, y_dev)
+
     @pl.when(y == w_y)
     def _():
         for k in range(NY - 1):
             remote(
                 w_hbm.at[w_rows, w_cols(y_to[k])], wfull.at[w_y, z], w1_send.at[k], w1_recv, y_dev[k]
             ).start()
-
-    fan_out(lambda k: parts_out.at[y_to[k]], parts_in.at[y], d1_send, d1_recv, y_dev)
 
     load_v.wait()
     for h in range(HEADS):
@@ -243,8 +246,8 @@
             lanes = slice(h * HD, (h + 1) * HD)
             qg_ref[b * RB : (b + 1) * RB, lanes] = qg_t[:, lanes].T.astype(BF16)
 
+    stores[0].start()
     stores[1].start()
-    stores[2].start()
 
     @pl.when(y == w_y)
     def _():
@@ -254,7 +257,11 @@
     def _():
         remote(wfull.at[w_y, z], wfull.at[w_y, z], w1_send.at[0], w1_recv, y_dev[0]).wait_recv()
 
-    fan_out(lambda k: wfull.at[w_y, z], wfull.at[w_y, z], wz_send, wz_recv, z_dev)
+    def chunk_part(i, j):
+        return wfull.at[w_y, j, :, pl.ds(*WEIGHT_PARTS[i])]
+
+    for i in range(2):
+        fan_out(lambda k: chunk_part(i, z), chunk_part(i, z), wz_send.at[i], wz_recv.at[i], z_dev)
 
     landed(lambda k: parts_in.at[y_from[k]], d1_send, d1_recv, y_dev)
     total_rows = parts_out[y].astype(F32)
@@ -266,14 +273,23 @@
     def summed(i):
         return jnp.concatenate([sums[:, i].reshape(NY * ROWS, HD).astype(F32), total_rows[2 + i]], axis=0)
 
-    def first_half(block):
-        return wfull.at[block, : NZ // 2]
-
-    def second_half(block):
-        return wfull.at[block, NZ // 2 :]
-
-    def send_core(k, block):
-        return remote(wfull.at[block], wfull.at[block], wc_send.at[k], wc_recv.at[k], sibling)
+    def block_part(i, block):
+        return wfull.at[block, :, :, pl.ds(*WEIGHT_PARTS[i])]
+
+    def send_along_x(i):
+        landed(lambda k: chunk_part(i, z_from[k]), wz_send.at[i], wz_recv.at[i], z_dev)
+        fan_out(lambda k: block_part(i, w_y), block_part(i, w_y), wx_send.at[i], wx_recv.at[i], x_dev)
+        send_core(i, 0, w_y).start()
+
+    def send_core(i, k, block):
+        ref = block_part(i, block)
+        return remote(ref, ref, wc_send.at[i, k], wc_recv.at[i, k], sibling)
+
+    def forward_to_core(i):
+        for k in range(NX - 1):
+            ref = block_part(i, 4 * c + x_from[k])
+            remote(ref, ref, wx_send.at[i, k], wx_recv.at[i, k], x_dev[k]).wait_recv()
+            send_core(i, 1 + k, 4 * c + x_from[k]).start()
 
     landed(lambda k: sums.at[y_from[k]], d2_send, d2_recv, y_dev)
     fan_out(lambda k: vgfull.at[y], vgfull.at[y], vg_send, vg_recv, y_dev)
@@ -284,9 +300,7 @@
     rs_src[NZ - 1] = over_tokens(summed(0), own_values).astype(BF16)
     fan_out(lambda k: rs_src.at[z_to[k]], rs_dst.at[z], rs_send, rs_recv, z_dev)
 
-    landed(lambda k: wfull.at[w_y, z_from[k]], wz_send, wz_recv, z_dev)
-    fan_out(lambda k: first_half(w_y), first_half(w_y), wx_send.at[0], wx_recv.at[0], x_dev)
-    send_core(0, w_y).start()
+    send_along_x(0)
 
     landed(lambda k: rs_dst.at[z_from[k]], rs_send, rs_recv, z_dev)
     total = rs_src[z].astype(F32)
@@ -294,36 +308,38 @@
         total = total + rs_dst[z_from[k]].astype(F32)
     bc_buf[x * NC + c] = total.astype(BF16)
     fan_out(lambda k: bc_buf.at[x * NC + c], bc_buf.at[x * NC + c], bc_send, bc_recv, xc_dev)
-    fan_out(lambda k: second_half(w_y), second_half(w_y), wx_send.at[1], wx_recv.at[1], x_dev)
+    send_along_x(1)
+
+    forward_to_core(0)
 
     landed(lambda k: bc_buf.at[xc_from[k][0] * NC + xc_from[k][1]], bc_send, bc_recv, xc_dev)
     total_ref[...] = sum_of(bc_buf).astype(BF16)
-    stores[3].start()
+    stores[2].start()
     fan_out(lambda k: total_ref, sums_hbm.at[z], ag_send, ag_recv, z_dev)
-    for k in range(NX - 1):
-        block = 4 * c + x_from[k]
-        for i, half in enumerate((first_half(block), second_half(block))):
-            remote(half, half, wx_send.at[i, k], wx_recv.at[i, k], x_dev[k]).wait_recv()
-        send_core(1 + k, block).start()
-
     landed(lambda k: vgfull.at[y_from[k]], vg_send, vg_recv, y_dev)
-    send_core(0, 4 * (1 - c) + x).wait_recv()
-    for k in range(NX - 1):
-        send_core(1 + k, 4 * (1 - c) + x_from[k]).wait_recv()
     values = jnp.concatenate([vgfull[j] for j in range(NY)], axis=1)
     up = up.astype(BF16)
-    for low, high in ((0, 256), (256, 512), (512, 768), (768, 896)):
-        frozen = dot(values, wfull[:, :, :, low:high].reshape(NY * HD, high - low))
-        down = at_ref[:, low:high]
-        for rows, factor in ((slice(0, HALF), first(down)), (slice(HALF, CTX), second(down))):
-            lig_ref[rows, low:high] = (frozen[rows] + adapter_scale * dot(up, factor)).astype(BF16)
-    stores[0].start()
+    for i in range(2):
+        send_core(i, 0, 4 * (1 - c) + x).wait_recv()
+        for k in range(NX - 1):
+            send_core(i, 1 + k, 4 * (1 - c) + x_from[k]).wait_recv()
+        start, size = WEIGHT_PARTS[i]
+        for low in range(start, start + size, 256):
+            high = min(low + 256, FEATS)
+            frozen = dot(values, wfull[:, :, :, low:high].reshape(NY * HD, high - low))
+            down = at_ref[:, low:high]
+            for rows, factor in ((slice(0, HALF), first(down)), (slice(HALF, CTX), second(down))):
+                lig_ref[rows, low:high] = (frozen[rows] + adapter_scale * dot(up, factor)).astype(BF16)
+        stores[3 + i].start()
+        if i == 0:
+            forward_to_core(1)
 
     landed(lambda k: sums_hbm.at[z_from[k]], ag_send, ag_recv, z_dev)
 
-    send_core(0, w_y).wait_send()
-    for k in range(NX - 1):
-        send_core(1 + k, 4 * c + x_from[k]).wait_send()
+    for i in range(2):
+        send_core(i, 0, w_y).wait_send()
+        for k in range(NX - 1):
+            send_core(i, 1 + k, 4 * c + x_from[k]).wait_send()
     for copy in pending:
         copy.wait_send()
     for store in stores:
@@ -419,15 +435,15 @@
             pltpu.VMEM((RESP, FEATS), BF16),
             pltpu.VMEM((CTX, HD), BF16),
             dma((10,)),
-            dma((4,)),
+            dma((5,)),
             dma((NY - 1,)),
             dma,
-            dma((NZ - 1,)),
-            dma((NZ - 1,)),
+            dma((2, NZ - 1)),
+            dma((2, NZ - 1)),
             dma((2, NX - 1)),
             dma((2, NX - 1)),
-            dma((NX,)),
-            dma((NX,)),
+            dma((2, NX)),
+            dma((2, NX)),
             dma((NY - 1,)),
             dma((NY - 1,)),
             dma((NY - 1,)),

time: 50 us -> 48 us (0.960)
  Pallas kernels: 48.5 us -> 46.5 us
    pallas_call x1, Pallas kernels: 46.3 us -> 44.3 us  [per_device(): pl.pallas_call(kernel, out_shape=(jax.ShapeDtypeStruct((CTX, FEATS), BF16...]
where the time goes in v6:
time: 48 us; the launch traced here: 47.8 us
  Pallas kernels  46.5 us (97%)
  between operations  1.29 us (3%)
    pallas_call x1, Pallas kernels, per_device(): pl.pallas_call(kernel, out_shape=(jax.ShapeDtypeStruct((CTX, FEATS), BF16...  44.3 us
    pallas_call x1, Pallas kernels, per_device(): pl.pallas_call(hand_on, out_shape=(jax.ShapeDtypeStruct((CTX, FEATS), BF1...  2.17 us

profile of v6, /device:TPU:1, one launch (start us, length us, event | category | flops | bytes accessed | tf_op | source)
XLA Modules:
  0.0 47.8 jit_solution(5460550315290001730)
XLA Ops:
  1.3 44.3 %shard_map.137 = (bf16[288,896]{1,0:T(8,128)(2,1)}, bf16[256,896]{1,0:T(8,128)(2,1)}, bf16[288,128]{1,0:T(8,128)(2,1)}, bf16[8,64,128]{2,1,0:T(8,128)(2,1)}) custom-call(bf16[288,896]{1,0:T(8,128)(2,1)} %x_hbm.1, bf16[256,896]{1,0:T(8,128)(2,1)} %q_hbm.1, bf16[288,128]{1,0:T(8,128)(2,1)} %k_hbm.1, bf16[288,128]{1,0:T(8,128)(2,1)} %v_hbm.1, ...), custom_call_target="tpu_custom_call" | custom-call | tf_op jit(solution)/shard_map/pallas_call | solution.py:401
  45.6 2.2 %shard_map.138 = (bf16[288,896]{1,0:T(8,128)(2,1)}, bf16[256,896]{1,0:T(8,128)(2,1)}, bf16[288,128]{1,0:T(8,128)(2,1)}, f32[64,896]{1,0:T(8,128)}, f32[64,128]{1,0:T(8,128)}) custom-call(bf16[288,896]{1,0:T(8,128)(2,1)} %get-tuple-element.14.lig_hbm, bf16[256,896]{1,0:T(8,128)(2,1)} %get-tuple-element.15.qg_hbm, bf16[288,128]{1,0:T(8,128)(2,1)} %get-tuple-element.16.kg_hbm, ...), custom_call_target="tpu_custom_call" | custom-call | tf_op jit(solution)/shard_map/pallas_call | solution.py:475

commit v7 on v6

--- a/solution.py
+++ b/solution.py
@@ -170,10 +170,8 @@
             total = total + parts[j].astype(F32)
         return total
 
-    load_k.wait()
-    load_q.wait()
-    load_mask.wait()
-    load_length.wait()
+    for load in (load_k, load_q, load_mask, load_length, load_x, load_a, load_g, load_b):
+        load.wait()
     limit = PROMPT - 1 + length_ref[0]
     probs = (p0, p1)
     probs_low = (pb0, pb1)
@@ -203,15 +201,11 @@
             parts_out[j, i] = rows[j * ROWS : (j + 1) * ROWS]
             parts_out[j, 2 + i] = rows[NY * ROWS :]
 
-    load_x.wait()
-    load_a.wait()
     hand_out(0, rank_rows(x_ref, at_ref[...]))
-    load_g.wait()
     early = dot(pb0[...], rows_of_heads(g_ref, 0))
     late = dot(pb1[...], rows_of_heads(g_ref, 1))
     vgfull[y, : SEEN[0], :] = (early + late[: SEEN[0]]).astype(BF16)
     vgfull[y, SEEN[0] :, :] = late[SEEN[0] :].astype(BF16)
-    load_b.wait()
     own_values = vgfull[y]
     hand_out(1, rank_rows(own_values, b_ref[...]))
 
@@ -225,6 +219,27 @@
             remote(
                 w_hbm.at[w_rows, w_cols(y_to[k])], wfull.at[w_y, z], w1_send.at[k], w1_recv, y_dev[k]
             ).start()
+
+    landed(lambda k: parts_in.at[y_from[k]], d1_send, d1_recv, y_dev)
+    total_rows = parts_out[y].astype(F32)
+    for k in range(NY - 1):
+        total_rows = total_rows + parts_in[y_from[k]].astype(F32)
+    sums[y] = total_rows[:2].astype(BF16)
+    fan_out(lambda k: sums.at[y], sums.at[y], d2_send, d2_recv, y_dev)
+
+    @pl.when(y == w_y)
+    def _():
+        w_own.wait()
+
+    @pl.when(y != w_y)
+    def _():
+        remote(wfull.at[w_y, z], wfull.at[w_y, z], w1_send.at[0], w1_recv, y_dev[0]).wait_recv()
+
+    def chunk_part(i, j):
+        return wfull.at[w_y, j, :, pl.ds(*WEIGHT_PARTS[i])]
+
+    for i in range(2):
+        fan_out(lambda k: chunk_part(i, z), chunk_part(i, z), wz_send.at[i], wz_recv.at[i], z_dev)
 
     load_v.wait()
     for h in range(HEADS):
@@ -248,27 +263,6 @@
 
     stores[0].start()
     stores[1].start()
-
-    @pl.when(y == w_y)
-    def _():
-        w_own.wait()
-
-    @pl.when(y != w_y)
-    def _():
-        remote(wfull.at[w_y, z], wfull.at[w_y, z], w1_send.at[0], w1_recv, y_dev[0]).wait_recv()
-
-    def chunk_part(i, j):
-        return wfull.at[w_y, j, :, pl.ds(*WEIGHT_PARTS[i])]
-
-    for i in range(2):
-        fan_out(lambda k: chunk_part(i, z), chunk_part(i, z), wz_send.at[i], wz_recv.at[i], z_dev)
-
-    landed(lambda k: parts_in.at[y_from[k]], d1_send, d1_recv, y_dev)
-    total_rows = parts_out[y].astype(F32)
-    for k in range(NY - 1):
-        total_rows = total_rows + parts_in[y_from[k]].astype(F32)
-    sums[y] = total_rows[:2].astype(BF16)
-    fan_out(lambda k: sums.at[y], sums.at[y], d2_send, d2_recv, y_dev)
 
     def summed(i):
         return jnp.concatenate([sums[:, i].reshape(NY * ROWS, HD).astype(F32), total_rows[2 + i]], axis=0)

time: 48 us -> 47.6 us (level)
  no operation moved by 1% of the time
where the time goes in v7:
time: 47.6 us; the launch traced here: 47.4 us
  Pallas kernels  46.1 us (97%)
  between operations  1.29 us (3%)
    pallas_call x1, Pallas kernels, per_device(): pl.pallas_call(kernel, out_shape=(jax.ShapeDtypeStruct((CTX, FEATS), BF16...  44 us
    pallas_call x1, Pallas kernels, per_device(): pl.pallas_call(hand_on, out_shape=(jax.ShapeDtypeStruct((CTX, FEATS), BF1...  2.17 us

profile of v7, /device:TPU:1, one launch (start us, length us, event | category | flops | bytes accessed | tf_op | source)
XLA Modules:
  0.0 47.4 jit_solution(15734528061036343880)
XLA Ops:
  1.3 44.0 %shard_map.137 = (bf16[288,896]{1,0:T(8,128)(2,1)}, bf16[256,896]{1,0:T(8,128)(2,1)}, bf16[288,128]{1,0:T(8,128)(2,1)}, bf16[8,64,128]{2,1,0:T(8,128)(2,1)}) custom-call(bf16[288,896]{1,0:T(8,128)(2,1)} %x_hbm.1, bf16[256,896]{1,0:T(8,128)(2,1)} %q_hbm.1, bf16[288,128]{1,0:T(8,128)(2,1)} %k_hbm.1, bf16[288,128]{1,0:T(8,128)(2,1)} %v_hbm.1, ...), custom_call_target="tpu_custom_call" | custom-call | tf_op jit(solution)/shard_map/pallas_call | solution.py:395
  45.3 2.2 %shard_map.138 = (bf16[288,896]{1,0:T(8,128)(2,1)}, bf16[256,896]{1,0:T(8,128)(2,1)}, bf16[288,128]{1,0:T(8,128)(2,1)}, f32[64,896]{1,0:T(8,128)}, f32[64,128]{1,0:T(8,128)}) custom-call(bf16[288,896]{1,0:T(8,128)(2,1)} %get-tuple-element.14.lig_hbm, bf16[256,896]{1,0:T(8,128)(2,1)} %get-tuple-element.15.qg_hbm, bf16[288,128]{1,0:T(8,128)(2,1)} %get-tuple-element.16.kg_hbm, ...), custom_call_target="tpu_custom_call" | custom-call | tf_op jit(solution)/shard_map/pallas_call | solution.py:469

commit v8 on v7

--- a/solution.py
+++ b/solution.py
@@ -241,6 +241,36 @@
     for i in range(2):
         fan_out(lambda k: chunk_part(i, z), chunk_part(i, z), wz_send.at[i], wz_recv.at[i], z_dev)
 
+    def summed(i):
+        return jnp.concatenate([sums[:, i].reshape(NY * ROWS, HD).astype(F32), total_rows[2 + i]], axis=0)
+
+    def block_part(i, block):
+        return wfull.at[block, :, :, pl.ds(*WEIGHT_PARTS[i])]
+
+    def send_along_x(i):
+        landed(lambda k: chunk_part(i, z_from[k]), wz_send.at[i], wz_recv.at[i], z_dev)
+        fan_out(lambda k: block_part(i, w_y), block_part(i, w_y), wx_send.at[i], wx_recv.at[i], x_dev)
+        send_core(i, 0, w_y).start()
+
+    def send_core(i, k, block):
+        ref = block_part(i, block)
+        return remote(ref, ref, wc_send.at[i, k], wc_recv.at[i, k], sibling)
+
+    def forward_to_core(i):
+        for k in range(NX - 1):
+            ref = block_part(i, 4 * c + x_from[k])
+            remote(ref, ref, wx_send.at[i, k], wx_recv.at[i, k], x_dev[k]).wait_recv()
+            send_core(i, 1 + k, 4 * c + x_from[k]).start()
+
+    landed(lambda k: sums.at[y_from[k]], d2_send, d2_recv, y_dev)
+    up = summed(1)
+    dfg_t = over_tokens(up, x_ref)
+    for j in range(NZ - 1):
+        rs_src[j] = dfg_t[:, j * 128 : (j + 1) * 128].astype(BF16)
+    rs_src[NZ - 1] = over_tokens(summed(0), own_values).astype(BF16)
+    fan_out(lambda k: rs_src.at[z_to[k]], rs_dst.at[z], rs_send, rs_recv, z_dev)
+    fan_out(lambda k: vgfull.at[y], vgfull.at[y], vg_send, vg_recv, y_dev)
+
     load_v.wait()
     for h in range(HEADS):
         for b in range(2):
@@ -263,36 +293,6 @@
 
     stores[0].start()
     stores[1].start()
-
-    def summed(i):
-        return jnp.concatenate([sums[:, i].reshape(NY * ROWS, HD).astype(F32), total_rows[2 + i]], axis=0)
-
-    def block_part(i, block):
-        return wfull.at[block, :, :, pl.ds(*WEIGHT_PARTS[i])]
-
-    def send_along_x(i):
-        landed(lambda k: chunk_part(i, z_from[k]), wz_send.at[i], wz_recv.at[i], z_dev)
-        fan_out(lambda k: block_part(i, w_y), block_part(i, w_y), wx_send.at[i], wx_recv.at[i], x_dev)
-        send_core(i, 0, w_y).start()
-
-    def send_core(i, k, block):
-        ref = block_part(i, block)
-        return remote(ref, ref, wc_send.at[i, k], wc_recv.at[i, k], sibling)
-
-    def forward_to_core(i):
-        for k in range(NX - 1):
-            ref = block_part(i, 4 * c + x_from[k])
-            remote(ref, ref, wx_send.at[i, k], wx_recv.at[i, k], x_dev[k]).wait_recv()
-            send_core(i, 1 + k, 4 * c + x_from[k]).start()
-
-    landed(lambda k: sums.at[y_from[k]], d2_send, d2_recv, y_dev)
-    fan_out(lambda k: vgfull.at[y], vgfull.at[y], vg_send, vg_recv, y_dev)
-    up = summed(1)
-    dfg_t = over_tokens(up, x_ref)
-    for j in range(NZ - 1):
-        rs_src[j] = dfg_t[:, j * 128 : (j + 1) * 128].astype(BF16)
-    rs_src[NZ - 1] = over_tokens(summed(0), own_values).astype(BF16)
-    fan_out(lambda k: rs_src.at[z_to[k]], rs_dst.at[z], rs_send, rs_recv, z_dev)
 
     send_along_x(0)
 

time: 47.6 us -> 47.6 us (level)
  no operation moved by 1% of the time
where the time goes in v8:
time: 47.6 us; the launch traced here: 47.4 us
  Pallas kernels  46.1 us (97%)
  between operations  1.29 us (3%)
    pallas_call x1, Pallas kernels, per_device(): pl.pallas_call(kernel, out_shape=(jax.ShapeDtypeStruct((CTX, FEATS), BF16...  43.9 us
    pallas_call x1, Pallas kernels, per_device(): pl.pallas_call(hand_on, out_shape=(jax.ShapeDtypeStruct((CTX, FEATS), BF1...  2.17 us

profile of v8, /device:TPU:1, one launch (start us, length us, event | category | flops | bytes accessed | tf_op | source)
XLA Modules:
  0.0 47.4 jit_solution(170692527097537021)
XLA Ops:
  1.3 43.9 %shard_map.137 = (bf16[288,896]{1,0:T(8,128)(2,1)}, bf16[256,896]{1,0:T(8,128)(2,1)}, bf16[288,128]{1,0:T(8,128)(2,1)}, bf16[8,64,128]{2,1,0:T(8,128)(2,1)}) custom-call(bf16[288,896]{1,0:T(8,128)(2,1)} %x_hbm.1, bf16[256,896]{1,0:T(8,128)(2,1)} %q_hbm.1, bf16[288,128]{1,0:T(8,128)(2,1)} %k_hbm.1, bf16[288,128]{1,0:T(8,128)(2,1)} %v_hbm.1, ...), custom_call_target="tpu_custom_call" | custom-call | tf_op jit(solution)/shard_map/pallas_call | solution.py:395
  45.2 2.2 %shard_map.138 = (bf16[288,896]{1,0:T(8,128)(2,1)}, bf16[256,896]{1,0:T(8,128)(2,1)}, bf16[288,128]{1,0:T(8,128)(2,1)}, f32[64,896]{1,0:T(8,128)}, f32[64,128]{1,0:T(8,128)}) custom-call(bf16[288,896]{1,0:T(8,128)(2,1)} %get-tuple-element.14.lig_hbm, bf16[256,896]{1,0:T(8,128)(2,1)} %get-tuple-element.15.qg_hbm, bf16[288,128]{1,0:T(8,128)(2,1)} %get-tuple-element.16.kg_hbm, ...), custom_call_target="tpu_custom_call" | custom-call | tf_op jit(solution)/shard_map/pallas_call | solution.py:469
